TPU v7x, 32 devices: a whole 2x2x4 slice. The times are simulated.
32 devices in a mesh: ctx: 16 (over z, x, core), head: 2 (over y).
Axes of the slice: x: 2, y: 2, z: 4, core: 2. Of those that a mesh axis runs over, the one named last changes fastest.
Arguments:
- queries: bfloat16 [4096, 2048], P('ctx', 'head'), as said below
- keys: bfloat16 [4096, 2048], P('ctx', 'head'), as said below
- values: bfloat16 [4096, 2048], P('ctx', 'head'), may hold values from -6 to 6
- dout: bfloat16 [4096, 2048], P('ctx', 'head'), may hold values from -6 to 6
- beacon_keys: bfloat16 [512, 2048], P('ctx', 'head'), may hold values from -6 to 6
- beacon_values: bfloat16 [512, 2048], P('ctx', 'head'), may hold values from -6 to 6
- beacon_key_weight: bfloat16 [4096, 2048], P('ctx', 'head'), may hold values from -0.125 to 0.125
- beacon_value_weight: bfloat16 [4096, 2048], P('ctx', 'head'), may hold values from -0.125 to 0.125
- lengths: int32 [16], replicated, may hold values from 1 to 256, as said below
- counts: int32 [16], replicated, may hold values from 1 to 32, as said below
Outputs:
- query_grad: bfloat16 [4096, 2048], P('ctx', 'head')
- key_grad: bfloat16 [4096, 2048], P('ctx', 'head')
- value_grad: bfloat16 [4096, 2048], P('ctx', 'head')
- beacon_key_grad: bfloat16 [512, 2048], P('ctx', 'head')
- beacon_value_grad: bfloat16 [512, 2048], P('ctx', 'head')
- beacon_hidden_grad: bfloat16 [512, 4096], P('ctx', 'head')
Inputs may be any that keep to these rules, and one draw needn't show every extreme that they name: `queries`: every entry lies in -10 to 10. `keys`: every entry lies in -10 to 10. `lengths`: some group has exactly 256 raw tokens in every draw. counts[c] = ceil(lengths[c] / 8).
All inputs are finite; a program needn't handle non-finite values.
Results may differ from a plain program's by a relative error of at most 0.019.
Values may be sent and summed in bfloat16 or wider, within the bound.
A program may use at most 64 MiB of HBM per device.

v0:
```python
import jax
import jax.numpy as jnp
from jax import lax
from jax.sharding import PartitionSpec as P

HEAD_DIM = 128


def group_masks(group_id, lengths, counts, rows, beacon_rows, per_group):
    group_ids = jnp.arange(lengths.shape[0], dtype=jnp.int32)
    length = jnp.sum(jnp.where(group_ids == group_id, lengths, 0))
    positions = jnp.arange(rows, dtype=jnp.int32)
    raw_mask = (positions[None, :] <= positions[:, None]) & (positions[None, :] < length)
    slots = jnp.arange(beacon_rows, dtype=jnp.int32)
    owners = slots // per_group
    owner_count = jnp.sum(
        jnp.where(owners[:, None] == group_ids[None, :], counts[None, :], 0), axis=1
    )
    beacon_mask = (owners < group_id) & (slots % per_group < owner_count)
    return (raw_mask, beacon_mask, positions < length)


def head_pass(qh, kh, vh, doh, bkh, bvh, raw_mask, beacon_mask, scale):
    rows = kh.shape[0]
    keys_all = jnp.concatenate([kh, bkh], axis=0)
    vals_all = jnp.concatenate([vh, bvh], axis=0)
    mask = jnp.concatenate(
        [raw_mask, jnp.broadcast_to(beacon_mask[None, :], (qh.shape[0], bkh.shape[0]))], axis=1
    )
    scores = jnp.einsum("td,sd->ts", qh, keys_all, preferred_element_type=jnp.float32) * scale
    scores = jnp.where(mask, scores, -jnp.inf)
    top = jnp.max(scores, axis=1, keepdims=True)
    expo = jnp.exp(scores - top)
    total = jnp.sum(expo, axis=1, keepdims=True)
    probs = expo / total
    probs_low = probs.astype(jnp.bfloat16)
    output = jnp.einsum("ts,sd->td", probs_low, vals_all, preferred_element_type=jnp.float32)
    delta = jnp.sum(doh.astype(jnp.float32) * output, axis=1, keepdims=True)
    dprobs = jnp.einsum("td,sd->ts", doh, vals_all, preferred_element_type=jnp.float32)
    dscores = (probs * (dprobs - delta) * scale).astype(jnp.bfloat16)
    dq = jnp.einsum("ts,sd->td", dscores, keys_all, preferred_element_type=jnp.float32).astype(
        jnp.bfloat16
    )
    dk = jnp.einsum("ts,td->sd", dscores[:, :rows], qh, preferred_element_type=jnp.float32).astype(
        jnp.bfloat16
    )
    dv = jnp.einsum(
        "ts,td->sd", probs_low[:, :rows], doh, preferred_element_type=jnp.float32
    ).astype(jnp.bfloat16)
    dkb = jnp.einsum("ts,td->sd", dscores[:, rows:], qh, preferred_element_type=jnp.float32)
    dvb = jnp.einsum("ts,td->sd", probs_low[:, rows:], doh, preferred_element_type=jnp.float32)
    return (dq, dk, dv, dkb, dvb, top, total, delta)


def run_job(task, all_keys, all_values, lengths, counts, per_group, scale):
    q_part, k_part, v_part, grad_part, group_id, column = task
    rows = q_part.shape[0]
    raw_mask, beacon_mask, valid = group_masks(
        group_id, lengths, counts, rows, all_keys.shape[0], per_group
    )
    grad_part = jnp.where(valid[:, None], grad_part, jnp.zeros_like(grad_part))
    dq_list, dk_list, dv_list, dkb_list, dvb_list, saved = ([], [], [], [], [], [])
    for head_slot in range(q_part.shape[1] // HEAD_DIM):
        local = slice(head_slot * HEAD_DIM, (head_slot + 1) * HEAD_DIM)
        lower = column + head_slot * HEAD_DIM
        qh = q_part[:, local]
        doh = grad_part[:, local]
        bkh = all_keys[:, lower : lower + HEAD_DIM]
        bvh = all_values[:, lower : lower + HEAD_DIM]
        dq, dk, dv, dkb, dvb, top, total, delta = head_pass(
            qh, k_part[:, local], v_part[:, local], doh, bkh, bvh, raw_mask, beacon_mask, scale
        )
        dq_list.append(dq)
        dk_list.append(dk)
        dv_list.append(dv)
        dkb_list.append(dkb)
        dvb_list.append(dvb)
        saved.append((qh, doh, top, total, delta, beacon_mask, lower))
    grads = (
        jnp.concatenate(dq_list, axis=1),
        jnp.concatenate(dk_list, axis=1),
        jnp.concatenate(dv_list, axis=1),
    )
    return (grads, dkb_list, dvb_list, saved)


def per_device(
    queries,
    keys,
    values,
    dout,
    beacon_keys,
    beacon_values,
    beacon_key_weight,
    beacon_value_weight,
    lengths,
    counts,
):
    width = queries.shape[1]
    per_group = beacon_keys.shape[0]
    scale = HEAD_DIM ** (-0.5)
    position = lax.axis_index("ctx")
    all_keys, all_values = (
        lax.all_gather(beacon_keys, "ctx", axis=0, tiled=True),
        lax.all_gather(beacon_values, "ctx", axis=0, tiled=True),
    )
    tasks = [(queries, keys, values, dout, position, 0)]
    results = [
        run_job(task, all_keys, all_values, lengths, counts, per_group, scale) for task in tasks
    ]
    dkb_parts = [part for result in results for part in result[1]]
    dvb_parts = [part for result in results for part in result[2]]
    terms = jnp.concatenate(dkb_parts + dvb_parts, axis=1)
    summed = lax.psum_scatter(terms, "ctx", scatter_dimension=0, tiled=True)
    own_grads = results[0][0]
    query_grad, key_grad, value_grad = own_grads
    beacon_key_grad = summed[:, :width].astype(jnp.bfloat16)
    beacon_value_grad = summed[:, width:].astype(jnp.bfloat16)
    weights = jnp.stack([beacon_key_weight, beacon_value_weight])
    piece = lax.all_gather(weights, "ctx", axis=1, tiled=True)
    first = lax.dot_general(
        beacon_key_grad, piece[0], (((1,), (1,)), ((), ())), preferred_element_type=jnp.float32
    )
    second = lax.dot_general(
        beacon_value_grad, piece[1], (((1,), (1,)), ((), ())), preferred_element_type=jnp.float32
    )
    partial_hidden = first + second
    hidden = lax.psum_scatter(
        partial_hidden.astype(jnp.bfloat16), "head", scatter_dimension=1, tiled=True
    )
    return (query_grad, key_grad, value_grad, beacon_key_grad, beacon_value_grad, hidden)


def solution(mesh):
    return jax.shard_map(
        per_device,
        mesh=mesh,
        in_specs=(
            P("ctx", "head"),
            P("ctx", "head"),
            P("ctx", "head"),
            P("ctx", "head"),
            P("ctx", "head"),
            P("ctx", "head"),
            P("ctx", "head"),
            P("ctx", "head"),
            P(),
            P(),
        ),
        out_specs=(
            P("ctx", "head"),
            P("ctx", "head"),
            P("ctx", "head"),
            P("ctx", "head"),
            P("ctx", "head"),
            P("ctx", "head"),
        ),
        check_vma=False,
    )
```

profile of v0, /device:TPU:0, one launch (start us, length us, event | category | flops | bytes accessed | tf_op | source)
XLA Modules:
  0.0 371.1 jit_solution(17112773755807289568)
XLA Ops:
  9.5 1.3 fusion.189
  10.8 1.2 copy.44
  12.8 1.8 fusion.228
  14.6 1.9 fusion.227
  16.6 34.2 %all-gather.4.cloned.1.call-done = bf16[512,1024]{1,0:T(8,128)(2,1)} async-done(((bf16[32,1024]{1,0:T(8,128)(2,1)}), bf16[512,1024]{1,0:T(8,128)(2,1)}) %all-gather.4.cloned.1.call-update) | async-done | bytes 1048592 | tf_op jit(solution)/shard_map/all_gather | solution.py:104
  50.8 1.4 fusion.225
  52.3 1.2 fusion.229
  53.8 36.0 %all-gather.6.cloned.1.call-done = bf16[512,1024]{1,0:T(8,128)(2,1)} async-done(((bf16[32,1024]{1,0:T(8,128)(2,1)}), bf16[512,1024]{1,0:T(8,128)(2,1)}) %all-gather.6.cloned.1.call-update) | async-done | bytes 1048592 | tf_op jit(solution)/shard_map/all_gather | solution.py:105
  89.9 1.4 fusion.224
  91.3 1.2 fusion.68
  92.5 1.1 fusion.36
  93.7 1.3 fusion.230
  95.3 1.2 fusion.69
  97.7 1.3 fusion.231
  99.3 1.2 fusion.70
  100.5 1.1 fusion.38
  101.6 1.2 fusion.232
  103.2 1.2 fusion.71
  104.4 1.1 fusion.39
  105.5 1.2 fusion.233
  107.1 1.2 fusion.72
  109.4 1.2 fusion.234
  111.0 1.3 fusion.73
  112.3 1.1 fusion.41
  113.5 1.2 fusion.235
  115.0 1.2 fusion.74
  117.4 1.3 fusion.236
  119.0 1.1 fusion.75
  120.2 1.2 fusion.43
  136.3 5.4 %copy.66 = f32[512,2048]{1,0:T(8,128)} copy(f32[512,2048]{0,1:T(8,128)} %convolution_dynamic-update-slice_fusion) | data formatting | bytes 8388608
  141.8 2.3 pad_maximum_fusion
  144.5 1.3 fusion.67
  147.7 1.1 fusion.65
  148.9 1.2 fusion.64
  150.1 1.1 fusion.63
  151.2 1.1 fusion.62
  152.3 1.1 fusion.61
  153.5 1.1 fusion.60
  157.9 1.7 fusion.54
  159.6 1.3 fusion.44
  163.1 50.3 %reduce-scatter.7.cloned.1.call-done = f32[32,2048]{1,0:T(8,128)} async-done(((f32[512,2048]{1,0:T(8,128)}), f32[32,2048]{1,0:T(8,128)}) %reduce-scatter.7.cloned.1.call-update) | async-done | bytes 262160
  213.4 1.2 copy.67
  214.7 127.2 %all-gather.8.cloned.1.call-done = bf16[2,4096,1024]{2,1,0:T(8,128)(2,1)} async-done(((bf16[2,256,1024]{2,1,0:T(8,128)(2,1)}), bf16[2,4096,1024]{2,1,0:T(8,128)(2,1)}) %all-gather.8.cloned.1.call-update) | async-done | bytes 16777232 | tf_op jit(solution)/shard_map/all_gather | solution.py:120
  341.8 6.0 %fusion = f32[32,4096]{1,0:T(8,128)S(1)} fusion(bf16[2,4096,1024]{2,1,0:T(8,128)(2,1)} %all-gather.8.cloned.1.call-done, bf16[32,2048]{0,1:T(8,128)(2,1)S(1)} %copy.67), kind=kOutput, calls=%fused_computation.1 | convolution fusion | flops 268435456 | bytes 9175040 | tf_op jit(solution)/shard_map/dot_general | solution.py:124
  347.8 6.7 %fusion.3 = bf16[32,4096]{1,0:T(8,128)(2,1)} fusion(f32[32,4096]{1,0:T(8,128)S(1)} %fusion, bf16[2,4096,1024]{2,1,0:T(8,128)(2,1)} %all-gather.8.cloned.1.call-done, bf16[32,2048]{0,1:T(8,128)(2,1)S(1)} %copy.67), kind=kOutput, calls=%fused_computation.5 | convolution fusion | flops 268697600 | bytes 9437184 | tf_op jit(solution)/shard_map/dot_general | solution.py:121
  356.4 2.0 copy.54
  359.3 2.0 copy.55
  362.8 1.7 reduce-scatter.5.cloned.1.call-done
  (179 shorter events, 35.6 us)
Async XLA Ops:
  7.2 43.7 %all-gather.4.cloned.1.call-start = ((), (), s32[]{:S(2)}) async-start(), calls=%async_computation.2 | async-start | bytes 1114112 | tf_op jit(solution)/shard_map/all_gather | solution.py:104
  7.9 82.0 %all-gather.6.cloned.1.call-start = ((), (), s32[]{:S(2)}) async-start(), calls=%async_computation.3 | async-start | bytes 1114112 | tf_op jit(solution)/shard_map/all_gather | solution.py:105
  8.6 204.8 %reduce-scatter.7.cloned.1.call-start = ((), (), s32[]{:S(2)}) async-start(), calls=%async_computation.6 | async-start | bytes 4456448
  12.8 41.0 %copy-start.52 = (pred[256,256]{0,1:T(32,128)(4,1)}, pred[256,256]{0,1:T(32,128)(4,1)S(1)}, u32[]{:S(2)}) copy-start(pred[256,256]{0,1:T(32,128)(4,1)S(1)} %fusion.108) | copy-start | bytes 196612
  14.6 39.3 %copy-start.44 = (bf16[256,128]{1,0:T(8,128)(2,1)}, bf16[256,128]{1,0:T(8,128)(2,1)S(1)}, u32[]{:S(2)}) copy-start(bf16[256,128]{1,0:T(8,128)(2,1)S(1)} %get-tuple-element.56) | copy-start | bytes 196612
  14.6 90.9 %copy-start.37 = (bf16[256,128]{1,0:T(8,128)(2,1)}, bf16[256,128]{1,0:T(8,128)(2,1)S(1)}, u32[]{:S(2)}) copy-start(bf16[256,128]{1,0:T(8,128)(2,1)S(1)} %get-tuple-element.52) | copy-start | bytes 196612
  14.6 94.8 %copy-start.35 = (bf16[256,128]{1,0:T(8,128)(2,1)}, bf16[256,128]{1,0:T(8,128)(2,1)S(1)}, u32[]{:S(2)}) copy-start(bf16[256,128]{1,0:T(8,128)(2,1)S(1)} %get-tuple-element.51) | copy-start | bytes 196612
  14.6 98.9 %copy-start.33 = (bf16[256,128]{1,0:T(8,128)(2,1)}, bf16[256,128]{1,0:T(8,128)(2,1)S(1)}, u32[]{:S(2)}) copy-start(bf16[256,128]{1,0:T(8,128)(2,1)S(1)} %get-tuple-element.57) | copy-start | bytes 196612
  14.6 102.8 %copy-start.31 = (bf16[256,128]{1,0:T(8,128)(2,1)}, bf16[256,128]{1,0:T(8,128)(2,1)S(1)}, u32[]{:S(2)}) copy-start(bf16[256,128]{1,0:T(8,128)(2,1)S(1)} %get-tuple-element.50) | copy-start | bytes 196612
  16.6 75.9 %copy-start = (bf16[256,1024]{0,1:T(8,128)(2,1)}, bf16[256,1024]{0,1:T(8,128)(2,1)S(1)}, u32[]{:S(2)}) copy-start(bf16[256,1024]{0,1:T(8,128)(2,1)S(1)} %broadcast_select_fusion) | copy-start | bytes 1572868
  52.2 41.4 %copy-start.30 = (bf16[512,128]{1,0:T(8,128)(2,1)}, bf16[512,128]{1,0:T(8,128)(2,1)S(1)}, u32[]{:S(2)}) copy-start(bf16[512,128]{1,0:T(8,128)(2,1)S(1)} %get-tuple-element.39) | copy-start | bytes 393220
  52.2 41.4 %copy-start.28 = (bf16[512,128]{1,0:T(8,128)(2,1)}, bf16[512,128]{1,0:T(8,128)(2,1)S(1)}, u32[]{:S(2)}) copy-start(bf16[512,128]{1,0:T(8,128)(2,1)S(1)} %get-tuple-element.38) | copy-start | bytes 393220
  52.2 45.4 %copy-start.26 = (bf16[512,128]{1,0:T(8,128)(2,1)}, bf16[512,128]{1,0:T(8,128)(2,1)S(1)}, u32[]{:S(2)}) copy-start(bf16[512,128]{1,0:T(8,128)(2,1)S(1)} %get-tuple-element.37) | copy-start | bytes 393220
  52.3 49.4 %copy-start.24 = (bf16[512,128]{1,0:T(8,128)(2,1)}, bf16[512,128]{1,0:T(8,128)(2,1)S(1)}, u32[]{:S(2)}) copy-start(bf16[512,128]{1,0:T(8,128)(2,1)S(1)} %get-tuple-element.36) | copy-start | bytes 393220
  52.3 53.3 %copy-start.22 = (bf16[512,128]{1,0:T(8,128)(2,1)}, bf16[512,128]{1,0:T(8,128)(2,1)S(1)}, u32[]{:S(2)}) copy-start(bf16[512,128]{1,0:T(8,128)(2,1)S(1)} %get-tuple-element.35) | copy-start | bytes 393220
  52.3 57.2 %copy-start.20 = (bf16[512,128]{1,0:T(8,128)(2,1)}, bf16[512,128]{1,0:T(8,128)(2,1)S(1)}, u32[]{:S(2)}) copy-start(bf16[512,128]{1,0:T(8,128)(2,1)S(1)} %get-tuple-element.34) | copy-start | bytes 393220
  93.6 27.7 %copy-start.5 = (bf16[256,768]{0,1:T(8,128)(2,1)}, bf16[256,768]{0,1:T(8,128)(2,1)S(1)}, u32[]{:S(2)}) copy-start(bf16[256,768]{0,1:T(8,128)(2,1)S(1)} %fusion.36) | copy-start | bytes 1179652
  97.6 24.7 %copy-start.6 = (bf16[256,768]{0,1:T(8,128)(2,1)}, bf16[256,768]{0,1:T(8,128)(2,1)S(1)}, u32[]{:S(2)}) copy-start(bf16[256,768]{0,1:T(8,128)(2,1)S(1)} %fusion.37) | copy-start | bytes 1179652
  101.6 21.6 %copy-start.8 = (bf16[256,768]{0,1:T(8,128)(2,1)}, bf16[256,768]{0,1:T(8,128)(2,1)S(1)}, u32[]{:S(2)}) copy-start(bf16[256,768]{0,1:T(8,128)(2,1)S(1)} %fusion.38) | copy-start | bytes 1179652
  105.5 18.6 %copy-start.10 = (bf16[256,768]{0,1:T(8,128)(2,1)}, bf16[256,768]{0,1:T(8,128)(2,1)S(1)}, u32[]{:S(2)}) copy-start(bf16[256,768]{0,1:T(8,128)(2,1)S(1)} %fusion.39) | copy-start | bytes 1179652
  109.4 15.7 %copy-start.12 = (bf16[256,768]{0,1:T(8,128)(2,1)}, bf16[256,768]{0,1:T(8,128)(2,1)S(1)}, u32[]{:S(2)}) copy-start(bf16[256,768]{0,1:T(8,128)(2,1)S(1)} %fusion.40) | copy-start | bytes 1179652
  111.0 22.6 %copy-start.2 = (bf16[256,768]{0,1:T(8,128)(2,1)}, bf16[256,768]{0,1:T(8,128)(2,1)S(1)}, u32[]{:S(2)}) copy-start(bf16[256,768]{0,1:T(8,128)(2,1)S(1)} %fusion.111) | copy-start | bytes 1179652
  113.4 12.6 %copy-start.14 = (bf16[256,768]{0,1:T(8,128)(2,1)}, bf16[256,768]{0,1:T(8,128)(2,1)S(1)}, u32[]{:S(2)}) copy-start(bf16[256,768]{0,1:T(8,128)(2,1)S(1)} %fusion.41) | copy-start | bytes 1179652
  117.3 9.6 %copy-start.16 = (bf16[256,768]{0,1:T(8,128)(2,1)}, bf16[256,768]{0,1:T(8,128)(2,1)S(1)}, u32[]{:S(2)}) copy-start(bf16[256,768]{0,1:T(8,128)(2,1)S(1)} %fusion.42) | copy-start | bytes 1179652
  120.1 8.7 %copy-start.1 = (bf16[256,1024]{0,1:T(8,128)(2,1)S(1)}, bf16[256,1024]{0,1:T(8,128)(2,1)}, u32[]{:S(2)}) copy-start(bf16[256,1024]{0,1:T(8,128)(2,1)} %copy-done) | copy-start | bytes 1572868
  121.3 14.0 %copy-start.18 = (bf16[256,768]{0,1:T(8,128)(2,1)}, bf16[256,768]{0,1:T(8,128)(2,1)S(1)}, u32[]{:S(2)}) copy-start(bf16[256,768]{0,1:T(8,128)(2,1)S(1)} %fusion.43) | copy-start | bytes 1179652
  141.7 200.1 %all-gather.8.cloned.1.call-start = ((), (), s32[]{:S(2)}) async-start(), calls=%async_computation.4 | async-start | bytes 17825792 | tf_op jit(solution)/shard_map/all_gather | solution.py:120
  144.1 220.5 %reduce-scatter.5.cloned.1.call-start = ((), (), s32[]{:S(2)}) async-start(), calls=%async_computation.5 | async-start | bytes 393216 | tf_op jit(solution)/shard_map/reduce_scatter | solution.py:128
  144.3 16.7 %copy-start.7 = (bf16[256,768]{0,1:T(8,128)(2,1)S(1)}, bf16[256,768]{0,1:T(8,128)(2,1)}, u32[]{:S(2)}) copy-start(bf16[256,768]{0,1:T(8,128)(2,1)} %copy-done.6) | copy-start | bytes 1179652
  144.3 16.7 %copy-start.29 = (bf16[512,128]{1,0:T(8,128)(2,1)S(1)}, bf16[512,128]{1,0:T(8,128)(2,1)}, u32[]{:S(2)}) copy-start(bf16[512,128]{1,0:T(8,128)(2,1)} %copy-done.28) | copy-start | bytes 393220
  144.3 16.7 %copy-start.43 = (bf16[256,128]{1,0:T(8,128)(2,1)S(1)}, bf16[256,128]{1,0:T(8,128)(2,1)}, u32[]{:S(2)}) copy-start(bf16[256,128]{1,0:T(8,128)(2,1)} %get-tuple-element.55) | copy-start | bytes 196612
  144.3 16.9 %copy-start.9 = (bf16[256,768]{0,1:T(8,128)(2,1)S(1)}, bf16[256,768]{0,1:T(8,128)(2,1)}, u32[]{:S(2)}) copy-start(bf16[256,768]{0,1:T(8,128)(2,1)} %copy-done.8) | copy-start | bytes 1179652
  144.3 16.9 %copy-start.27 = (bf16[512,128]{1,0:T(8,128)(2,1)S(1)}, bf16[512,128]{1,0:T(8,128)(2,1)}, u32[]{:S(2)}) copy-start(bf16[512,128]{1,0:T(8,128)(2,1)} %copy-done.26) | copy-start | bytes 393220
  144.4 16.9 %copy-start.42 = (bf16[256,128]{1,0:T(8,128)(2,1)S(1)}, bf16[256,128]{1,0:T(8,128)(2,1)}, u32[]{:S(2)}) copy-start(bf16[256,128]{1,0:T(8,128)(2,1)} %get-tuple-element.54) | copy-start | bytes 196612
  144.4 17.2 %copy-start.11 = (bf16[256,768]{0,1:T(8,128)(2,1)S(1)}, bf16[256,768]{0,1:T(8,128)(2,1)}, u32[]{:S(2)}) copy-start(bf16[256,768]{0,1:T(8,128)(2,1)} %copy-done.10) | copy-start | bytes 1179652
  144.4 17.2 %copy-start.25 = (bf16[512,128]{1,0:T(8,128)(2,1)S(1)}, bf16[512,128]{1,0:T(8,128)(2,1)}, u32[]{:S(2)}) copy-start(bf16[512,128]{1,0:T(8,128)(2,1)} %copy-done.24) | copy-start | bytes 393220
  144.4 17.2 %copy-start.40 = (bf16[256,128]{1,0:T(8,128)(2,1)S(1)}, bf16[256,128]{1,0:T(8,128)(2,1)}, u32[]{:S(2)}) copy-start(bf16[256,128]{1,0:T(8,128)(2,1)} %get-tuple-element.53) | copy-start | bytes 196612
  144.4 17.5 %copy-start.13 = (bf16[256,768]{0,1:T(8,128)(2,1)S(1)}, bf16[256,768]{0,1:T(8,128)(2,1)}, u32[]{:S(2)}) copy-start(bf16[256,768]{0,1:T(8,128)(2,1)} %copy-done.12) | copy-start | bytes 1179652
  144.4 17.5 %copy-start.23 = (bf16[512,128]{1,0:T(8,128)(2,1)S(1)}, bf16[512,128]{1,0:T(8,128)(2,1)}, u32[]{:S(2)}) copy-start(bf16[512,128]{1,0:T(8,128)(2,1)} %copy-done.22) | copy-start | bytes 393220
  144.4 17.5 %copy-start.38 = (bf16[256,128]{1,0:T(8,128)(2,1)S(1)}, bf16[256,128]{1,0:T(8,128)(2,1)}, u32[]{:S(2)}) copy-start(bf16[256,128]{1,0:T(8,128)(2,1)} %copy-done.37) | copy-start | bytes 196612
  144.4 17.8 %copy-start.15 = (bf16[256,768]{0,1:T(8,128)(2,1)S(1)}, bf16[256,768]{0,1:T(8,128)(2,1)}, u32[]{:S(2)}) copy-start(bf16[256,768]{0,1:T(8,128)(2,1)} %copy-done.14) | copy-start | bytes 1179652
  144.4 17.8 %copy-start.21 = (bf16[512,128]{1,0:T(8,128)(2,1)S(1)}, bf16[512,128]{1,0:T(8,128)(2,1)}, u32[]{:S(2)}) copy-start(bf16[512,128]{1,0:T(8,128)(2,1)} %copy-done.20) | copy-start | bytes 393220
  144.5 17.8 %copy-start.36 = (bf16[256,128]{1,0:T(8,128)(2,1)S(1)}, bf16[256,128]{1,0:T(8,128)(2,1)}, u32[]{:S(2)}) copy-start(bf16[256,128]{1,0:T(8,128)(2,1)} %copy-done.35) | copy-start | bytes 196612
  145.7 16.7 %copy-start.17 = (bf16[256,768]{0,1:T(8,128)(2,1)S(1)}, bf16[256,768]{0,1:T(8,128)(2,1)}, u32[]{:S(2)}) copy-start(bf16[256,768]{0,1:T(8,128)(2,1)} %copy-done.16) | copy-start | bytes 1179652
  145.7 16.7 %copy-start.34 = (bf16[256,128]{1,0:T(8,128)(2,1)S(1)}, bf16[256,128]{1,0:T(8,128)(2,1)}, u32[]{:S(2)}) copy-start(bf16[256,128]{1,0:T(8,128)(2,1)} %copy-done.33) | copy-start | bytes 196612
  148.9 13.9 %copy-start.19 = (bf16[256,768]{0,1:T(8,128)(2,1)S(1)}, bf16[256,768]{0,1:T(8,128)(2,1)}, u32[]{:S(2)}) copy-start(bf16[256,768]{0,1:T(8,128)(2,1)} %copy-done.18) | copy-start | bytes 1179652
  148.9 13.9 %copy-start.32 = (bf16[256,128]{1,0:T(8,128)(2,1)S(1)}, bf16[256,128]{1,0:T(8,128)(2,1)}, u32[]{:S(2)}) copy-start(bf16[256,128]{1,0:T(8,128)(2,1)} %copy-done.31) | copy-start | bytes 196612
  154.6 8.2 %copy-start.4 = (bf16[256,1024]{0,1:T(8,128)(2,1)}, bf16[256,1024]{0,1:T(8,128)(2,1)S(1)}, u32[]{:S(2)}) copy-start(bf16[256,1024]{0,1:T(8,128)(2,1)S(1)} %fusion.60) | copy-start | bytes 1572868
  (11 other events, 43.4 us)
Sparse Core Ops, SparseCore 0:
  10.2 40.6 all-gather.3
  53.0 36.8 all-gather.5
  141.8 71.5 reduce-scatter.6
  215.7 126.0 all-gather.7
  354.7 9.8 reduce-scatter.4
where the time goes:
time: 373 us; the launch traced here: 371 us
  waiting for transfers between devices  251 us (67%)
  matrix products  76.1 us (20%)
  local copies, waits for them, and re-layouts  21.2 us (6%)
  between operations  14.9 us (4%)
  other arithmetic  7.54 us (2%)
    all_gather x1, waiting for transfers between devices, per_device(): piece = lax.all_gather(weights, 'ctx', axis=1, tiled=True)  127 us
    unnamed x6, waiting for transfers between devices  51.8 us
    all_gather x1, waiting for transfers between devices, per_device(): lax.all_gather(beacon_values, 'ctx', axis=0, tiled=True)  36 us
    all_gather x1, waiting for transfers between devices, per_device(): lax.all_gather(beacon_keys, 'ctx', axis=0, tiled=True)  34.2 us
    unnamed x116, local copies, waits for them, and re-layouts  14.7 us
    dot_general x8, matrix products, head_pass(): jnp.einsum('td,sd->ts', qh, keys_all, preferred_element_type=jnp.float32)  10.1 us
    dot_general x8, matrix products, head_pass(): jnp.einsum('ts,sd->td', probs_low, vals_all, preferred_element_type=jnp.f...  9.36 us
    dot_general x8, matrix products, head_pass(): jnp.einsum('ts,td->sd', dscores[:, :rows], qh, preferred_element_type=jnp...  9.24 us
  transfers between devices with their start and end apart: 5, of which 5 were waited for; matrix products, arithmetic and copies ran while one was open for 11% of the time, Pallas kernels for 0%

commit v1 on v0

v1 whole, which is shorter than its diff:
```python
import functools

import jax
import jax.numpy as jnp
from jax import lax
from jax.experimental import pallas as pl
from jax.experimental.pallas import tpu as pltpu
from jax.sharding import PartitionSpec as P

HEAD_DIM = 128
LOG2E = 1.4426950408889634
NEG = -1e30


def dot_nt(a, b):
    return lax.dot_general(a, b, (((1,), (1,)), ((), ())), preferred_element_type=jnp.float32)


def dot_nn(a, b):
    return lax.dot_general(a, b, (((1,), (0,)), ((), ())), preferred_element_type=jnp.float32)


def dot_tn(a, b):
    return lax.dot_general(a, b, (((0,), (0,)), ((), ())), preferred_element_type=jnp.float32)


def fill_bias(bias, lengths_ref, counts_ref, me, rows, n_groups, per_group):
    length = lengths_ref[me]
    key_slot = lax.broadcasted_iota(jnp.int32, (rows, rows), 0)
    query_slot = lax.broadcasted_iota(jnp.int32, (rows, rows), 1)
    raw = (key_slot <= query_slot) & (key_slot < length)
    bias[0:rows, :] = jnp.where(raw, 0.0, NEG)
    slot = lax.broadcasted_iota(jnp.int32, (per_group, rows), 0)

    def one(group, carry):
        count = jnp.where(group < me, counts_ref[group], 0)
        at = pl.multiple_of(rows + group * per_group, per_group)
        bias[pl.ds(at, per_group), :] = jnp.where(slot < count, 0.0, NEG)
        return carry

    lax.fori_loop(0, n_groups, one, 0)


def attention_kernel(
    n_groups, lengths_ref, counts_ref, q_ref, k_ref, v_ref, g_ref, bk_ref, bv_ref,
    dq_ref, dk_ref, dv_ref, dkb_ref, dvb_ref, bias,
):
    rows, width = q_ref.shape
    per_group = bk_ref.shape[0] // n_groups
    me = lax.axis_index("ctx")
    fill_bias(bias, lengths_ref, counts_ref, me, rows, n_groups, per_group)
    scale = HEAD_DIM**-0.5
    valid = lax.broadcasted_iota(jnp.int32, (rows, HEAD_DIM), 0) < lengths_ref[me]

    for head in range(width // HEAD_DIM):
        cols = slice(head * HEAD_DIM, (head + 1) * HEAD_DIM)
        q = q_ref[:, cols]
        g = jnp.where(valid, g_ref[:, cols], jnp.zeros((rows, HEAD_DIM), jnp.bfloat16))
        keys = jnp.concatenate([k_ref[:, cols], bk_ref[:, cols]], axis=0)
        vals = jnp.concatenate([v_ref[:, cols], bv_ref[:, cols]], axis=0)
        scores = dot_nt(keys, q) * (scale * LOG2E) + bias[...]
        top = jnp.max(scores, axis=0, keepdims=True)
        expo = jnp.exp2(scores - top)
        total = jnp.sum(expo, axis=0, keepdims=True)
        probs = expo * (1.0 / total)
        low = probs.astype(jnp.bfloat16)
        dprobs = dot_nt(vals, g)
        delta = jnp.sum(low.astype(jnp.float32) * dprobs, axis=0, keepdims=True)
        dscores = (probs * ((dprobs - delta) * scale)).astype(jnp.bfloat16)
        dq_ref[:, cols] = dot_tn(keys, dscores).T.astype(jnp.bfloat16)
        dkeys = dot_nn(dscores, q)
        dvals = dot_nn(low, g)
        dk_ref[:, cols] = dkeys[:rows].astype(jnp.bfloat16)
        dv_ref[:, cols] = dvals[:rows].astype(jnp.bfloat16)
        dkb_ref[:, cols] = dkeys[rows:].astype(jnp.bfloat16)
        dvb_ref[:, cols] = dvals[rows:].astype(jnp.bfloat16)


def attention(q, k, v, g, bk, bv, lengths, counts):
    n_groups = lengths.shape[0]
    rows, width = q.shape
    slots = bk.shape[0]
    vmem = pl.BlockSpec(memory_space=pltpu.VMEM)
    smem = pl.BlockSpec(memory_space=pltpu.SMEM)
    low = jnp.bfloat16
    raw = jax.ShapeDtypeStruct((rows, width), low)
    beacon = jax.ShapeDtypeStruct((slots, width), low)
    return pl.pallas_call(
        functools.partial(attention_kernel, n_groups),
        out_shape=(raw, raw, raw, beacon, beacon),
        in_specs=[smem, smem] + [vmem] * 6,
        out_specs=(vmem,) * 5,
        scratch_shapes=[pltpu.VMEM((rows + slots, rows), jnp.float32)],
        compiler_params=pltpu.CompilerParams(vmem_limit_bytes=48 * 1024 * 1024),
    )(lengths, counts, q, k, v, g, bk, bv)


def per_device(
    queries,
    keys,
    values,
    dout,
    beacon_keys,
    beacon_values,
    beacon_key_weight,
    beacon_value_weight,
    lengths,
    counts,
):
    width = queries.shape[1]
    both = jnp.concatenate([beacon_keys, beacon_values], axis=1)
    gathered = lax.all_gather(both, "ctx", axis=0, tiled=True)
    query_grad, key_grad, value_grad, dkb, dvb = attention(
        queries, keys, values, dout, gathered[:, :width], gathered[:, width:], lengths, counts
    )
    terms = jnp.concatenate([dkb, dvb], axis=1)
    summed = lax.psum_scatter(terms, "ctx", scatter_dimension=0, tiled=True)
    all_grads = lax.all_gather(summed, "ctx", axis=0, tiled=True)
    weights = jnp.concatenate([beacon_key_weight, beacon_value_weight], axis=1)
    part = dot_nt(all_grads, weights).astype(jnp.bfloat16)
    mine = lax.all_to_all(part, "ctx", split_axis=0, concat_axis=1, tiled=True)
    hidden = lax.psum_scatter(mine, "head", scatter_dimension=1, tiled=True)
    return (query_grad, key_grad, value_grad, summed[:, :width], summed[:, width:], hidden)


def solution(mesh):
    spec = P("ctx", "head")
    return jax.shard_map(
        per_device,
        mesh=mesh,
        in_specs=(spec,) * 8 + (P(), P()),
        out_specs=(spec,) * 6,
        check_vma=False,
    )
```

time: 373 us -> 206 us (0.55)
  waiting for transfers between devices: 251 us -> 159 us
  matrix products: 76.1 us -> 2.34 us
  local copies, waits for them, and re-layouts: 21.2 us -> 4.12 us
  blocking collectives: 0 us -> 13.3 us
  Pallas kernels: 0 us -> 9.98 us
  other arithmetic: 7.54 us -> 3.06 us
    all_gather x3 -> x2, waiting for transfers between devices: 197 us -> 88.7 us  [the longest x1 46 us: per_device(): gathered = lax.all_gather(both, 'ctx', axis=0, tiled=True)]
    dot_general x66 -> x1, matrix products: 76.1 us -> 2.34 us  [dot_nt(): lax.dot_general(a, b, (((1,), (1,)), ((), ())), preferred_element_type=jn...]
    reduce_scatter x1 -> x2, waiting for transfers between devices: 1.72 us -> 69.9 us  [the longest x1 60.5 us: per_device(): summed = lax.psum_scatter(terms, 'ctx', scatter_dimension=0, tiled=True)]
    unnamed x6 -> x4, waiting for transfers between devices: 51.8 us -> 0.07 us
    unnamed x116 -> x18, local copies, waits for them, and re-layouts: 14.7 us -> 0.05 us
    all_to_all x0 -> x1, blocking collectives: none -> 13.3 us  [per_device(): mine = lax.all_to_all(part, 'ctx', split_axis=0, concat_axis=1, tiled=True)]
    pallas_call x0 -> x1, Pallas kernels: none -> 9.98 us  [attention(): pl.pallas_call(functools.partial(attention_kernel, n_groups), out_shape=(...]
  transfers between devices with their start and end apart: 5 -> 4, of which waited for: 5 -> 4; matrix products, arithmetic and copies ran while one was open for 11% -> 0% of each run, Pallas kernels for 0% -> 0%
where the time goes in v1:
time: 206 us
  waiting for transfers between devices  159 us (77%)
  between operations  13.9 us (7%)
  blocking collectives  13.3 us (6%)
  Pallas kernels  9.98 us (5%)
  local copies, waits for them, and re-layouts  4.12 us (2%)
  other arithmetic  3.06 us (1%)
  matrix products  2.34 us (1%)
    reduce_scatter x1, waiting for transfers between devices, per_device(): summed = lax.psum_scatter(terms, 'ctx', scatter_dimension=0, tiled=True)  60.5 us
    all_gather x1, waiting for transfers between devices, per_device(): gathered = lax.all_gather(both, 'ctx', axis=0, tiled=True)  46 us
    all_gather x1, waiting for transfers between devices, per_device(): all_grads = lax.all_gather(summed, 'ctx', axis=0, tiled=True)  42.7 us
    all_to_all x1, blocking collectives, per_device(): mine = lax.all_to_all(part, 'ctx', split_axis=0, concat_axis=1, tiled=True)  13.3 us
    pallas_call x1, Pallas kernels, attention(): pl.pallas_call(functools.partial(attention_kernel, n_groups), out_shape=(...  9.98 us
    reduce_scatter x1, waiting for transfers between devices, per_device(): hidden = lax.psum_scatter(mine, 'head', scatter_dimension=1, tiled=True)  9.42 us
  transfers between devices with their start and end apart: 4, of which 4 were waited for; matrix products, arithmetic and copies ran while one was open for 0% of the time, Pallas kernels for 0%

profile of v1, /device:TPU:0, one launch (start us, length us, event | category | flops | bytes accessed | tf_op | source)
XLA Modules:
  0.0 205.5 jit_solution(14854441415026097960)
XLA Ops:
  7.2 0.0 all-gather.3.cloned.1.call-start
  7.2 1.5 pad_maximum_fusion.1
  8.7 0.0 all-gather.3.cloned.1.call-update
  8.8 0.0 copy-start
  8.8 0.0 copy-start.1
  8.8 0.0 copy-start.2
  8.8 0.0 copy-start.3
  8.8 0.0 copy-start.4
  8.8 0.0 copy-start.5
  8.8 0.0 reduce-scatter.3.cloned.1.call-start
  8.9 46.0 %all-gather.3.cloned.1.call-done = bf16[512,2048]{1,0:T(8,128)(2,1)} async-done(((bf16[32,2048]{1,0:T(8,128)(2,1)}), bf16[512,2048]{1,0:T(8,128)(2,1)}) %all-gather.3.cloned.1.call-update) | async-done | bytes 2097168 | tf_op jit(solution)/shard_map/all_gather | solution.py:112
  54.9 2.7 %fusion.4 = (bf16[512,1024]{1,0:T(8,128)(2,1)}, bf16[512,1024]{1,0:T(8,128)(2,1)S(1)}) fusion(bf16[512,2048]{1,0:T(8,128)(2,1)} %all-gather.3.cloned.1.call-done), kind=kLoop, calls=%fused_computation.7 | loop fusion | bytes 4194304 | tf_op jit(solution)/shard_map/slice | solution.py:114
  57.5 0.0 copy-done
  57.6 0.0 copy-done.1
  57.6 0.0 copy-done.2
  57.6 0.0 copy-done.3
  57.6 0.0 copy-done.4
  57.6 0.0 copy-done.5
  57.6 10.0 %shard_map.145 = (bf16[256,1024]{1,0:T(8,128)(2,1)}, bf16[256,1024]{1,0:T(8,128)(2,1)}, bf16[256,1024]{1,0:T(8,128)(2,1)}, bf16[512,1024]{1,0:T(8,128)(2,1)S(1)}, bf16[512,1024]{1,0:T(8,128)(2,1)S(1)}) custom-call(s32[16]{0:T(128)S(1)} %copy-done.4, s32[16]{0:T(128)S(1)} %copy-done.5, bf16[256,1024]{1,0:T(8,128)(2,1)S(1)} %copy-done, ...), custom_call_target="tpu_custom_call" | custom-call | tf_op jit(solution)/shard_map/pallas_call | solution.py:88
  67.6 1.5 pad_maximum_fusion
  69.1 0.0 copy-start.7
  69.1 0.0 copy-start.8
  69.1 0.0 reduce-scatter.3.cloned.1.call-update
  69.1 0.0 all-gather.5.cloned.1.call-start
  69.2 60.5 %reduce-scatter.3.cloned.1.call-done = bf16[32,2048]{1,0:T(8,128)(2,1)} async-done(((bf16[512,2048]{1,0:T(8,128)(2,1)}), bf16[32,2048]{1,0:T(8,128)(2,1)}) %reduce-scatter.3.cloned.1.call-update) | async-done | bytes 131088 | tf_op jit(solution)/shard_map/reduce_scatter | solution.py:117
  129.7 0.0 all-gather.5.cloned.1.call-update
  129.7 0.0 copy-start.6
  129.7 0.0 reduce-scatter.5.cloned.1.call-start
  129.7 42.7 %all-gather.5.cloned.1.call-done = bf16[512,2048]{1,0:T(8,128)(2,1)} async-done(((bf16[32,2048]{1,0:T(8,128)(2,1)}), bf16[512,2048]{1,0:T(8,128)(2,1)}) %all-gather.5.cloned.1.call-update) | async-done | bytes 2097168 | tf_op jit(solution)/shard_map/all_gather | solution.py:118
  172.5 0.0 copy-done.7
  172.5 0.0 copy-done.8
  172.5 2.3 %convolution_convert_fusion = bf16[512,256]{1,0:T(8,128)(2,1)S(1)} fusion(bf16[512,2048]{1,0:T(8,128)(2,1)} %all-gather.5.cloned.1.call-done, bf16[256,1024]{1,0:T(8,128)(2,1)S(1)} %copy-done.7, bf16[256,1024]{1,0:T(8,128)(2,1)S(1)} %copy-done.8), kind=kOutput, calls=%fused_computation.1 | convolution fusion | flops 539099136 | bytes 3407872 | tf_op jit(solution)/shard_map/dot_general | solution.py:16
  174.8 13.3 %all_to_all.19 = bf16[16,32,256]{2,1,0:T(8,128)(2,1)S(1)} all-to-all(bf16[16,32,256]{2,1,0:T(8,128)(2,1)S(1)} %bitcast.7), channel_id=1, replica_groups=mesh['ctx'=16,'head'=2] {'ctx'}, dimensions={0} | all-to-all | bytes 524288 | tf_op jit(solution)/shard_map/all_to_all | solution.py:121
  188.1 0.7 copy.17
  188.9 0.0 reduce-scatter.5.cloned.1.call-update
  188.9 0.0 copy-done.6
  188.9 0.7 fusion.5
  189.6 9.4 %reduce-scatter.5.cloned.1.call-done = bf16[32,2048]{1,0:T(8,128)(2,1)} async-done(((bf16[32,4096]{1,0:T(8,128)(2,1)}), bf16[32,2048]{1,0:T(8,128)(2,1)}) %reduce-scatter.5.cloned.1.call-update) | async-done | bytes 131088 | tf_op jit(solution)/shard_map/reduce_scatter | solution.py:122
Async XLA Ops:
  7.2 47.7 %all-gather.3.cloned.1.call-start = ((), (), s32[]{:S(2)}) async-start(), calls=%async_computation.3 | async-start | bytes 2228224 | tf_op jit(solution)/shard_map/all_gather | solution.py:112
  8.8 48.8 %copy-start = (bf16[256,1024]{1,0:T(8,128)(2,1)S(1)}, bf16[256,1024]{1,0:T(8,128)(2,1)}, u32[]{:S(2)}) copy-start(bf16[256,1024]{1,0:T(8,128)(2,1)} %q_ref.1) | copy-start | bytes 1572868
  8.8 48.8 %copy-start.1 = (bf16[256,1024]{1,0:T(8,128)(2,1)S(1)}, bf16[256,1024]{1,0:T(8,128)(2,1)}, u32[]{:S(2)}) copy-start(bf16[256,1024]{1,0:T(8,128)(2,1)} %k_ref.1) | copy-start | bytes 1572868
  8.8 48.8 %copy-start.2 = (bf16[256,1024]{1,0:T(8,128)(2,1)S(1)}, bf16[256,1024]{1,0:T(8,128)(2,1)}, u32[]{:S(2)}) copy-start(bf16[256,1024]{1,0:T(8,128)(2,1)} %v_ref.1) | copy-start | bytes 1572868
  8.8 48.8 %copy-start.3 = (bf16[256,1024]{1,0:T(8,128)(2,1)S(1)}, bf16[256,1024]{1,0:T(8,128)(2,1)}, u32[]{:S(2)}) copy-start(bf16[256,1024]{1,0:T(8,128)(2,1)} %g_ref.1) | copy-start | bytes 1572868
  8.8 48.8 %copy-start.4 = (s32[16]{0:T(128)S(1)}, s32[16]{0:T(128)}, u32[]{:S(2)}) copy-start(s32[16]{0:T(128)} %lengths_ref.1) | copy-start | bytes 196
  8.8 48.7 %copy-start.5 = (s32[16]{0:T(128)S(1)}, s32[16]{0:T(128)}, u32[]{:S(2)}) copy-start(s32[16]{0:T(128)} %counts_ref.1) | copy-start | bytes 196
  8.8 120.8 %reduce-scatter.3.cloned.1.call-start = ((), (), s32[]{:S(2)}) async-start(), calls=%async_computation.4 | async-start | bytes 2228224 | tf_op jit(solution)/shard_map/reduce_scatter | solution.py:117
  69.1 103.4 %copy-start.7 = (bf16[256,1024]{1,0:T(8,128)(2,1)S(1)}, bf16[256,1024]{1,0:T(8,128)(2,1)}, u32[]{:S(2)}) copy-start(bf16[256,1024]{1,0:T(8,128)(2,1)} %param.17) | copy-start | bytes 1572868
  69.1 103.4 %copy-start.8 = (bf16[256,1024]{1,0:T(8,128)(2,1)S(1)}, bf16[256,1024]{1,0:T(8,128)(2,1)}, u32[]{:S(2)}) copy-start(bf16[256,1024]{1,0:T(8,128)(2,1)} %param.16) | copy-start | bytes 1572868
  69.1 103.3 %all-gather.5.cloned.1.call-start = ((), (), s32[]{:S(2)}) async-start(), calls=%async_computation.5 | async-start | bytes 2228224 | tf_op jit(solution)/shard_map/all_gather | solution.py:118
  129.7 59.2 %copy-start.6 = (bf16[32,2048]{1,0:T(8,128)(2,1)S(1)}, bf16[32,2048]{1,0:T(8,128)(2,1)}, u32[]{:S(2)}) copy-start(bf16[32,2048]{1,0:T(8,128)(2,1)} %reduce-scatter.3.cloned.1.call-done) | copy-start | bytes 393220
  129.7 69.3 %reduce-scatter.5.cloned.1.call-start = ((), (), s32[]{:S(2)}) async-start(), calls=%async_computation.6 | async-start | bytes 393216 | tf_op jit(solution)/shard_map/reduce_scatter | solution.py:122
Sparse Core Ops, SparseCore 0:
  10.7 44.0 all-gather.2
  69.2 60.3 reduce-scatter.2
  132.1 40.3 all-gather.4
  189.0 9.9 reduce-scatter.4

commit v2 on v1

v2 whole, which is shorter than its diff:
```python
import functools

import jax
import jax.numpy as jnp
from jax import lax
from jax.experimental import pallas as pl
from jax.experimental.pallas import tpu as pltpu
from jax.sharding import PartitionSpec as P

HEAD_DIM = 128
LOG2E = 1.4426950408889634
NEG = -1e30


def dot_nt(a, b):
    return lax.dot_general(a, b, (((1,), (1,)), ((), ())), preferred_element_type=jnp.float32)


def dot_nn(a, b):
    return lax.dot_general(a, b, (((1,), (0,)), ((), ())), preferred_element_type=jnp.float32)


def dot_tn(a, b):
    return lax.dot_general(a, b, (((0,), (0,)), ((), ())), preferred_element_type=jnp.float32)


def fill_bias(bias, lengths_ref, counts_ref, me, rows, n_groups, per_group):
    length = lengths_ref[me]
    key_slot = lax.broadcasted_iota(jnp.int32, (rows, rows), 0)
    query_slot = lax.broadcasted_iota(jnp.int32, (rows, rows), 1)
    raw = (key_slot <= query_slot) & (key_slot < length)
    bias[0:rows, :] = jnp.where(raw, 0.0, NEG)
    slot = lax.broadcasted_iota(jnp.int32, (per_group, rows), 0)

    def one(group, carry):
        count = jnp.where(group < me, counts_ref[group], 0)
        at = pl.multiple_of(rows + group * per_group, per_group)
        bias[pl.ds(at, per_group), :] = jnp.where(slot < count, 0.0, NEG)
        return carry

    lax.fori_loop(0, n_groups, one, 0)


def attention_kernel(
    n_groups, lengths_ref, counts_ref, q_ref, k_ref, v_ref, g_ref, beacon_ref,
    dq_ref, dk_ref, dv_ref, terms_ref, bias,
):
    rows, width = q_ref.shape
    per_group = beacon_ref.shape[0] // n_groups
    me = lax.axis_index("ctx")
    fill_bias(bias, lengths_ref, counts_ref, me, rows, n_groups, per_group)
    scale = HEAD_DIM**-0.5
    valid = lax.broadcasted_iota(jnp.int32, (rows, HEAD_DIM), 0) < lengths_ref[me]

    for head in range(width // HEAD_DIM):
        cols = slice(head * HEAD_DIM, (head + 1) * HEAD_DIM)
        q = q_ref[:, cols]
        g = jnp.where(valid, g_ref[:, cols], jnp.zeros((rows, HEAD_DIM), jnp.bfloat16))
        late = slice(width + head * HEAD_DIM, width + (head + 1) * HEAD_DIM)
        keys = jnp.concatenate([k_ref[:, cols], beacon_ref[:, cols]], axis=0)
        vals = jnp.concatenate([v_ref[:, cols], beacon_ref[:, late]], axis=0)
        scores = dot_nt(keys, q) * (scale * LOG2E) + bias[...]
        top = jnp.max(scores, axis=0, keepdims=True)
        expo = jnp.exp2(scores - top)
        total = jnp.sum(expo, axis=0, keepdims=True)
        probs = expo * (1.0 / total)
        low = probs.astype(jnp.bfloat16)
        dprobs = dot_nt(vals, g)
        delta = jnp.sum(low.astype(jnp.float32) * dprobs, axis=0, keepdims=True)
        dscores = (probs * ((dprobs - delta) * scale)).astype(jnp.bfloat16)
        dq_ref[:, cols] = dot_tn(keys, dscores).T.astype(jnp.bfloat16)
        dkeys = dot_nn(dscores, q)
        dvals = dot_nn(low, g)
        dk_ref[:, cols] = dkeys[:rows].astype(jnp.bfloat16)
        dv_ref[:, cols] = dvals[:rows].astype(jnp.bfloat16)
        terms_ref[:, cols] = dkeys[rows:].astype(jnp.bfloat16)
        terms_ref[:, late] = dvals[rows:].astype(jnp.bfloat16)


def attention(q, k, v, g, beacons, lengths, counts):
    n_groups = lengths.shape[0]
    rows, width = q.shape
    slots = beacons.shape[0]
    vmem = pl.BlockSpec(memory_space=pltpu.VMEM)
    smem = pl.BlockSpec(memory_space=pltpu.SMEM)
    raw = jax.ShapeDtypeStruct((rows, width), jnp.bfloat16)
    return pl.pallas_call(
        functools.partial(attention_kernel, n_groups),
        out_shape=(raw, raw, raw, jax.ShapeDtypeStruct(beacons.shape, jnp.bfloat16)),
        in_specs=[smem, smem] + [vmem] * 5,
        out_specs=(vmem,) * 4,
        scratch_shapes=[pltpu.VMEM((rows + slots, rows), jnp.float32)],
        compiler_params=pltpu.CompilerParams(vmem_limit_bytes=48 * 1024 * 1024),
    )(lengths, counts, q, k, v, g, beacons)


class Grid:
    def __init__(self, n):
        self.C = 2
        chips = n // 2
        self.X = 1
        while self.X * self.X * 4 <= chips:
            self.X *= 2
        self.Z = chips // self.X
        self.me = lax.axis_index("ctx")
        self.c = lax.rem(self.me, 2)
        self.x = lax.rem(self.me // 2, self.X)
        self.z = self.me // (2 * self.X)
        self.up, self.down = self.me + 2 * self.X, self.me - 2 * self.X
        self.partner = self.me + 1 - 2 * self.c

    def at(self, z, x, c):
        return (z * self.X + x) * 2 + c

    def greet(self):
        barrier = pltpu.get_barrier_semaphore()

        def hello(ctx):
            pl.semaphore_signal(
                barrier, inc=1, device_id={"ctx": ctx}, device_id_type=pl.DeviceIdType.MESH
            )

        hello(self.partner)
        for dx in range(1, self.X):
            hello(self.at(self.z, lax.rem(self.x + dx, self.X), self.c))
        pl.when(self.z < self.Z - 1)(lambda: hello(self.up))
        pl.when(self.z > 0)(lambda: hello(self.down))
        ends = jnp.where(self.z > 0, 1, 0) + jnp.where(self.z < self.Z - 1, 1, 0)
        return barrier, self.X + ends


def remote(src, dst, send, recv, ctx, head=None):
    where = {"ctx": ctx} if head is None else {"ctx": ctx, "head": head}
    return pltpu.make_async_remote_copy(
        src_ref=src, dst_ref=dst, send_sem=send, recv_sem=recv,
        device_id=where, device_id_type=pl.DeviceIdType.MESH,
    )


def spread_blocks(grid, buf, recv, z_send, x_send, c_send, both_ways):
    Z, X, z, x, c = grid.Z, grid.X, grid.z, grid.x, grid.c

    def copy(i, send, ctx):
        return remote(buf.at[i], buf.at[i], send, recv.at[i], ctx)

    def arrived(i):
        copy(i, c_send.at[i], grid.partner).wait_recv()

    def along_x(i, dx):
        return copy(i, x_send.at[i, dx - 1], grid.at(z, lax.rem(x + dx, X), c))

    def along_core(i):
        return copy(i, c_send.at[i], grid.partner)

    def along_z(i, upward):
        return copy(i, z_send.at[i, 0 if upward else 1], grid.up if upward else grid.down)

    def onward(zb, upward, downward, act):
        i = grid.at(zb, x, c)
        if upward:
            pl.when(z < Z - 1)(lambda: act(along_z(i, True)))
        if downward:
            pl.when(z > 0)(lambda: act(along_z(i, False)))
        for dx in range(1, X):
            act(along_x(i, dx))
        act(along_core(i))

    def column(s, act, wait):
        def lower():
            if wait:
                arrived(grid.at(z - s, x, c))
            onward(z - s, True, False, act)

        def upper():
            if wait:
                arrived(grid.at(z + s, x, c))
            onward(z + s, False, True, act)

        pl.when(z - s >= 0)(lower)
        if both_ways:
            pl.when(z + s < Z)(upper)

    def cross(s, act, wait):
        def row(zb):
            for dx in range(1, X):
                i = grid.at(zb, lax.rem(x + dx, X), c)
                if wait:
                    arrived(i)
                act(along_core(i))

        if s == 0:
            row(z)
            return
        pl.when(z - s >= 0)(lambda: row(z - s))
        if both_ways:
            pl.when(z + s < Z)(lambda: row(z + s))

    def start(d):
        d.start()

    def sent(d):
        d.wait_send()

    onward(z, True, both_ways, start)
    for s in range(1, Z):
        column(s, start, True)
        cross(s - 1, start, True)
    cross(Z - 1, start, True)

    def last(zb):
        for xb in range(X):
            arrived(grid.at(zb, xb, 1 - c))

    for zb in range(Z):
        if both_ways:
            last(zb)
        else:
            pl.when(zb <= z)(functools.partial(last, zb))

    def drain():
        onward(z, True, both_ways, sent)
        for s in range(1, Z):
            column(s, sent, False)
            cross(s - 1, sent, False)
        cross(Z - 1, sent, False)

    return drain


def gather_kernel(n, bk_ref, bv_ref, out_ref, recv, z_send, x_send, c_send):
    grid = Grid(n)
    width = bk_ref.shape[1]
    barrier, neighbours = grid.greet()
    out_ref[grid.me, :, 0:width] = bk_ref[...]
    out_ref[grid.me, :, width : 2 * width] = bv_ref[...]
    row = grid.X * grid.C

    for zb in range(1, grid.Z):

        def clear(zb=zb):
            part = out_ref.shape[1:]
            out_ref[zb * row : (zb + 1) * row] = jnp.zeros((row,) + part, out_ref.dtype)

        pl.when(zb > grid.z)(clear)
    pl.semaphore_wait(barrier, neighbours)
    spread_blocks(grid, out_ref, recv, z_send, x_send, c_send, False)()


def spread_sems(n):
    grid_x = 1
    while grid_x * grid_x * 4 <= n // 2:
        grid_x *= 2
    dma = pltpu.SemaphoreType.DMA
    return [dma((n,)), dma((n, 2)), dma((n, max(grid_x - 1, 1))), dma((n,))]


def gather_beacons(n, bk, bv):
    rows, width = bk.shape
    vmem = pl.BlockSpec(memory_space=pltpu.VMEM)
    return pl.pallas_call(
        functools.partial(gather_kernel, n),
        out_shape=jax.ShapeDtypeStruct((n, rows, 2 * width), jnp.bfloat16),
        in_specs=[vmem, vmem],
        out_specs=vmem,
        scratch_shapes=spread_sems(n),
        compiler_params=pltpu.CompilerParams(
            collective_id=0, has_side_effects=True, vmem_limit_bytes=48 * 1024 * 1024
        ),
    )(bk, bv)


def reduce_kernel(
    n, n_heads, terms_ref, wk_ref, wv_ref, own_ref, hidden_ref,
    grads, core_in, x_out, x_in, z_out, z_in, acc, h_out, h_in,
    recv, z_send, x_send, c_send, core_sem, xr_sem, zr_sem, h_send, h_recv,
):
    grid = Grid(n)
    Z, X, z, x, c, me = grid.Z, grid.X, grid.z, grid.x, grid.c, grid.me
    head = lax.axis_index("head")
    per_head = n // n_heads
    to_head = me // per_head
    width = wk_ref.shape[1]
    f32 = jnp.float32

    barrier, count = grid.greet()

    def hello(j, carry):
        src_c, src_h = head * per_head + j // n_heads, lax.rem(j, n_heads)

        @pl.when((src_c != me) | (src_h != head))
        def _():
            pl.semaphore_signal(
                barrier, inc=1, device_id={"ctx": src_c, "head": src_h},
                device_id_type=pl.DeviceIdType.MESH,
            )

        return carry

    lax.fori_loop(0, n, hello, 0)
    pl.semaphore_wait(barrier, count + n - jnp.where(to_head == head, 1, 0))

    def to_core(zb, xb):
        j = zb * X + xb
        return remote(
            terms_ref.at[grid.at(zb, xb, 1 - c)], core_in.at[j],
            core_sem.at[0, j], core_sem.at[1, j], grid.partner,
        )

    def to_x(zb, dx):
        return remote(
            x_out.at[zb, dx - 1], x_in.at[zb, dx - 1],
            xr_sem.at[0, zb, dx - 1], xr_sem.at[1, zb, dx - 1],
            grid.at(z, lax.rem(x + dx, X), c),
        )

    def to_z(zb):
        return remote(z_out.at[zb], z_in.at[zb], zr_sem.at[0, zb], zr_sem.at[1, zb], grid.down)

    def each_row(act):
        for zb in range(Z):
            pl.when(zb <= z)(functools.partial(act, zb))

    def core_row(zb):
        for dx in range(X):
            to_core(zb, lax.rem(x + dx, X)).start()

    each_row(core_row)

    def x_row(zb):
        for dx in list(range(1, X)) + [0]:
            xb = lax.rem(x + dx, X)
            to_core(zb, xb).wait_recv()
            total = terms_ref[grid.at(zb, xb, c)].astype(f32) + core_in[zb * X + xb].astype(f32)
            if dx == 0:
                acc[zb] = total
            else:
                x_out[zb, dx - 1] = total.astype(jnp.bfloat16)
                to_x(zb, dx).start()

    each_row(x_row)

    def z_row(zb):
        total = acc[zb]
        for dx in range(1, X):
            to_x(zb, dx).wait_recv()
            total = total + x_in[zb, dx - 1].astype(f32)
        acc[zb] = total

        @pl.when(z < Z - 1)
        def _():
            to_z(zb).wait_recv()
            acc[zb] = acc[zb] + z_in[zb].astype(f32)

        @pl.when(zb < z)
        def _():
            z_out[zb] = acc[zb].astype(jnp.bfloat16)
            to_z(zb).start()

        @pl.when(zb == z)
        def _():
            grads[me] = acc[zb].astype(jnp.bfloat16)

    each_row(z_row)
    own_ref[...] = grads[me]
    drain = spread_blocks(grid, grads, recv, z_send, x_send, c_send, True)

    rows = own_ref.shape[0]
    row = X * 2
    my_slot = (me - to_head * per_head) * n_heads + head

    def to_owner(b):
        return remote(h_out.at[b], h_in.at[my_slot], h_send.at[b], h_recv.at[my_slot], b, to_head)

    for zb in range(Z):
        block = grads[zb * row : (zb + 1) * row].reshape(row * rows, 2 * width)
        part = dot_nt(block[:, :width], wk_ref[...]) + dot_nt(block[:, width:], wv_ref[...])
        h_out[zb * row : (zb + 1) * row] = part.astype(jnp.bfloat16).reshape(row, rows, -1)

        def send(j, carry, zb=zb):
            b = zb * row + j
            here = (b == me) & (to_head == head)

            @pl.when(here)
            def _():
                h_in[my_slot] = h_out[b]

            @pl.when(jnp.logical_not(here))
            def _():
                to_owner(b).start()

            return carry

        lax.fori_loop(0, row, send, 0)

    def landed(j, carry):
        src_c, src_h = head * per_head + j // n_heads, lax.rem(j, n_heads)

        @pl.when((src_c != me) | (src_h != head))
        def _():
            remote(h_out.at[0], h_in.at[j], h_send.at[0], h_recv.at[j], me, head).wait_recv()

        return carry

    lax.fori_loop(0, n, landed, 0)
    cols = wk_ref.shape[0]
    for j in range(per_head):
        total = h_in[j * n_heads].astype(f32)
        for h in range(1, n_heads):
            total = total + h_in[j * n_heads + h].astype(f32)
        hidden_ref[:, j * cols : (j + 1) * cols] = total.astype(jnp.bfloat16)

    drain()

    def sent_row(zb):
        for dx in range(X):
            to_core(zb, lax.rem(x + dx, X)).wait_send()
        for dx in range(1, X):
            to_x(zb, dx).wait_send()
        pl.when(zb < z)(lambda: to_z(zb).wait_send())

    each_row(sent_row)

    def sent(b, carry):
        pl.when((b != me) | (to_head != head))(lambda: to_owner(b).wait_send())
        return carry

    lax.fori_loop(0, n, sent, 0)


def reduce_beacons(n, n_heads, terms, wk, wv):
    _, rows, both = terms.shape
    cols, width = wk.shape
    vmem = pl.BlockSpec(memory_space=pltpu.VMEM)
    low, dma = jnp.bfloat16, pltpu.SemaphoreType.DMA
    sems = spread_sems(n)
    X = 1
    while X * X * 4 <= n // 2:
        X *= 2
    Z, others = n // 2 // X, max(X - 1, 1)
    return pl.pallas_call(
        functools.partial(reduce_kernel, n, n_heads),
        out_shape=(
            jax.ShapeDtypeStruct((rows, both), low),
            jax.ShapeDtypeStruct((rows, cols * (n // n_heads)), low),
        ),
        in_specs=[vmem] * 3,
        out_specs=(vmem, vmem),
        scratch_shapes=[
            pltpu.VMEM((n, rows, both), low),
            pltpu.VMEM((Z * X, rows, both), low),
            pltpu.VMEM((Z, others, rows, both), low),
            pltpu.VMEM((Z, others, rows, both), low),
            pltpu.VMEM((Z, rows, both), low),
            pltpu.VMEM((Z, rows, both), low),
            pltpu.VMEM((Z, rows, both), jnp.float32),
            pltpu.VMEM((n, rows, cols), low),
            pltpu.VMEM((n, rows, cols), low),
        ]
        + sems
        + [dma((2, Z * X)), dma((2, Z, others)), dma((2, Z)), dma((n,)), dma((n,))],
        compiler_params=pltpu.CompilerParams(
            collective_id=1, has_side_effects=True, vmem_limit_bytes=48 * 1024 * 1024
        ),
    )(terms, wk, wv)


def per_device(
    n_heads,
    queries,
    keys,
    values,
    dout,
    beacon_keys,
    beacon_values,
    beacon_key_weight,
    beacon_value_weight,
    lengths,
    counts,
):
    n = lengths.shape[0]
    rows, width = beacon_keys.shape
    gathered = gather_beacons(n, beacon_keys, beacon_values)
    query_grad, key_grad, value_grad, terms = attention(
        queries, keys, values, dout, gathered.reshape(n * rows, 2 * width), lengths, counts
    )
    own, hidden = reduce_beacons(
        n, n_heads, terms.reshape(n, rows, 2 * width), beacon_key_weight, beacon_value_weight
    )
    return (query_grad, key_grad, value_grad, own[:, :width], own[:, width:], hidden)


def solution(mesh):
    spec = P("ctx", "head")
    return jax.shard_map(
        functools.partial(per_device, mesh.shape["head"]),
        mesh=mesh,
        in_specs=(spec,) * 8 + (P(), P()),
        out_specs=(spec,) * 6,
        check_vma=False,
    )
```

time: 206 us -> 82.4 us (0.40)
  waiting for transfers between devices: 159 us -> 0 us
  Pallas kernels: 9.98 us -> 75.8 us
  blocking collectives: 13.3 us -> 0 us
  between operations: 13.9 us -> 0.73 us
  other arithmetic: 3.06 us -> 0 us
  matrix products: 2.34 us -> 0 us
    all_gather x2 -> x0, waiting for transfers between devices: 88.7 us -> none  [the longest x1 46 us: per_device(): gathered = lax.all_gather(both, 'ctx', axis=0, tiled=True)]
    reduce_scatter x2 -> x0, waiting for transfers between devices: 69.9 us -> none  [the longest x1 60.5 us: per_device(): summed = lax.psum_scatter(terms, 'ctx', scatter_dimension=0, tiled=True)]
    pallas_call x0 -> x2, Pallas kernels: none -> 65.4 us  [the longest x1 56 us: reduce_beacons(): pl.pallas_call(functools.partial(reduce_kernel, n, n_heads), out_shape=(j...]
    all_to_all x1 -> x0, blocking collectives: 13.3 us -> none  [per_device(): mine = lax.all_to_all(part, 'ctx', split_axis=0, concat_axis=1, tiled=True)]
    unnamed x18 -> x23, local copies, waits for them, and re-layouts: 0.05 us -> 3.8 us
    concatenate x2 -> x0, other arithmetic: 3.06 us -> none  [the longest x1 1.54 us: per_device(): both = jnp.concatenate([beacon_keys, beacon_values], axis=1)]
    slice x2 -> x1, local copies, waits for them, and re-layouts: 3.34 us -> 0.66 us  [per_device(): own[:, width:]]
    dot_general x1 -> x0, matrix products: 2.34 us -> none  [dot_nt(): lax.dot_general(a, b, (((1,), (1,)), ((), ())), preferred_element_type=jn...]
  transfers between devices with their start and end apart: 4 -> 0, of which waited for: 4 -> 0; matrix products, arithmetic and copies ran while one was open for 0% -> 0% of each run, Pallas kernels for 0% -> 0%
where the time goes in v2:
time: 82.4 us; the launch traced here: 81 us
  Pallas kernels  75.8 us (92%)
  local copies, waits for them, and re-layouts  4.46 us (5%)
    pallas_call x1, Pallas kernels, reduce_beacons(): pl.pallas_call(functools.partial(reduce_kernel, n, n_heads), out_shape=(j...  56 us
    pallas_call x1, Pallas kernels, attention(): pl.pallas_call(functools.partial(attention_kernel, n_groups), out_shape=(...  10.4 us
    pallas_call x1, Pallas kernels, gather_beacons(): pl.pallas_call(functools.partial(gather_kernel, n), out_shape=jax.ShapeDt...  9.43 us
    unnamed x23, local copies, waits for them, and re-layouts  3.8 us

profile of v2, /device:TPU:0, one launch (start us, length us, event | category | flops | bytes accessed | tf_op | source)
XLA Modules:
  0.0 81.0 jit_solution(14270748791568895739)
XLA Ops:
  0.6 0.0 copy-start.4
  0.6 0.0 copy-start.3
  0.7 0.0 copy-start.2
  0.7 0.0 copy-start.7
  0.7 0.9 %copy-done.7 = bf16[32,1024]{1,0:T(8,128)(2,1)S(1)} copy-done((bf16[32,1024]{1,0:T(8,128)(2,1)S(1)}, bf16[32,1024]{1,0:T(8,128)(2,1)}, u32[]{:S(2)}) %copy-start.7) | copy-done | bytes 65560
  1.6 0.0 copy-start.8
  1.6 0.8 %copy-done.8 = bf16[32,1024]{1,0:T(8,128)(2,1)S(1)} copy-done((bf16[32,1024]{1,0:T(8,128)(2,1)S(1)}, bf16[32,1024]{1,0:T(8,128)(2,1)}, u32[]{:S(2)}) %copy-start.8) | copy-done | bytes 65560
  2.5 0.0 copy-start.1
  2.5 0.0 copy-start.9
  2.5 0.0 copy-start.10
  2.5 9.4 %shard_map.145 = bf16[16,32,2048]{2,1,0:T(8,128)(2,1)S(1)} custom-call(bf16[32,1024]{1,0:T(8,128)(2,1)S(1)} %copy-done.7, bf16[32,1024]{1,0:T(8,128)(2,1)S(1)} %copy-done.8), custom_call_target="tpu_custom_call" | custom-call | tf_op jit(solution)/shard_map/pallas_call | solution.py:260
  11.9 0.0 copy-start
  11.9 1.3 %copy-done = bf16[16,32,2048]{2,1,0:T(8,128)(2,1)} copy-done((bf16[16,32,2048]{2,1,0:T(8,128)(2,1)}, bf16[16,32,2048]{2,1,0:T(8,128)(2,1)S(1)}, u32[]{:S(2)}) %copy-start) | copy-done | bytes 2097176
  13.2 0.0 copy-done.4
  13.2 0.0 copy-done.3
  13.2 0.0 copy-done.2
  13.2 0.0 copy-done.1
  13.2 0.0 copy-done.9
  13.3 0.0 copy-done.10
  13.3 0.0 copy-start.5
  13.3 0.0 copy-start.6
  13.3 10.4 %shard_map.146 = (bf16[256,1024]{1,0:T(8,128)(2,1)}, bf16[256,1024]{1,0:T(8,128)(2,1)}, bf16[256,1024]{1,0:T(8,128)(2,1)}, bf16[512,2048]{1,0:T(8,128)(2,1)S(1)}) custom-call(s32[16]{0:T(128)S(1)} %copy-done.9, s32[16]{0:T(128)S(1)} %copy-done.10, bf16[256,1024]{1,0:T(8,128)(2,1)S(1)} %copy-done.1, bf16[256,1024]{1,0:T(8,128)(2,1)S(1)} %copy-done.2, ...), custom_call_target="tpu_custom_call" | custom-call | tf_op jit(solution)/shard_map/pallas_call | solution.py:87
  23.7 0.0 copy-done.5
  23.7 0.0 copy-done.6
  23.7 56.0 %shard_map.147 = (bf16[32,2048]{1,0:T(8,128)(2,1)S(1)}, bf16[32,2048]{1,0:T(8,128)(2,1)S(1)}) custom-call(bf16[16,32,2048]{2,1,0:T(8,128)(2,1)S(1)} %bitcast.3, bf16[256,1024]{1,0:T(8,128)(2,1)S(1)} %copy-done.5, bf16[256,1024]{1,0:T(8,128)(2,1)S(1)} %copy-done.6), custom_call_target="tpu_custom_call" | custom-call | tf_op jit(solution)/shard_map/pallas_call | solution.py:440
  79.7 0.7 fusion
  80.4 0.7 copy.17
Async XLA Ops:
  0.6 12.6 %copy-start.4 = (bf16[256,1024]{1,0:T(8,128)(2,1)S(1)}, bf16[256,1024]{1,0:T(8,128)(2,1)}, u32[]{:S(2)}) copy-start(bf16[256,1024]{1,0:T(8,128)(2,1)} %g_ref.1) | copy-start | bytes 1572868
  0.6 12.6 %copy-start.3 = (bf16[256,1024]{1,0:T(8,128)(2,1)S(1)}, bf16[256,1024]{1,0:T(8,128)(2,1)}, u32[]{:S(2)}) copy-start(bf16[256,1024]{1,0:T(8,128)(2,1)} %v_ref.1) | copy-start | bytes 1572868
  0.7 12.6 %copy-start.2 = (bf16[256,1024]{1,0:T(8,128)(2,1)S(1)}, bf16[256,1024]{1,0:T(8,128)(2,1)}, u32[]{:S(2)}) copy-start(bf16[256,1024]{1,0:T(8,128)(2,1)} %k_ref.1) | copy-start | bytes 1572868
  0.7 1.0 %copy-start.7 = (bf16[32,1024]{1,0:T(8,128)(2,1)S(1)}, bf16[32,1024]{1,0:T(8,128)(2,1)}, u32[]{:S(2)}) copy-start(bf16[32,1024]{1,0:T(8,128)(2,1)} %bk_ref.1) | copy-start | bytes 196612
  1.6 0.8 %copy-start.8 = (bf16[32,1024]{1,0:T(8,128)(2,1)S(1)}, bf16[32,1024]{1,0:T(8,128)(2,1)}, u32[]{:S(2)}) copy-start(bf16[32,1024]{1,0:T(8,128)(2,1)} %bv_ref.1) | copy-start | bytes 196612
  2.5 10.8 %copy-start.1 = (bf16[256,1024]{1,0:T(8,128)(2,1)S(1)}, bf16[256,1024]{1,0:T(8,128)(2,1)}, u32[]{:S(2)}) copy-start(bf16[256,1024]{1,0:T(8,128)(2,1)} %q_ref.1) | copy-start | bytes 1572868
  2.5 10.8 %copy-start.9 = (s32[16]{0:T(128)S(1)}, s32[16]{0:T(128)}, u32[]{:S(2)}) copy-start(s32[16]{0:T(128)} %lengths_ref.1) | copy-start | bytes 196
  2.5 10.8 %copy-start.10 = (s32[16]{0:T(128)S(1)}, s32[16]{0:T(128)}, u32[]{:S(2)}) copy-start(s32[16]{0:T(128)} %counts_ref.1) | copy-start | bytes 196
  11.9 1.3 %copy-start = (bf16[16,32,2048]{2,1,0:T(8,128)(2,1)}, bf16[16,32,2048]{2,1,0:T(8,128)(2,1)S(1)}, u32[]{:S(2)}) copy-start(bf16[16,32,2048]{2,1,0:T(8,128)(2,1)S(1)} %shard_map.145) | copy-start | bytes 6291460
  13.3 10.5 %copy-start.5 = (bf16[256,1024]{1,0:T(8,128)(2,1)S(1)}, bf16[256,1024]{1,0:T(8,128)(2,1)}, u32[]{:S(2)}) copy-start(bf16[256,1024]{1,0:T(8,128)(2,1)} %wk_ref.1) | copy-start | bytes 1572868
  13.3 10.4 %copy-start.6 = (bf16[256,1024]{1,0:T(8,128)(2,1)S(1)}, bf16[256,1024]{1,0:T(8,128)(2,1)}, u32[]{:S(2)}) copy-start(bf16[256,1024]{1,0:T(8,128)(2,1)} %wv_ref.1) | copy-start | bytes 1572868

commit v3 on v1

v3 whole, which is shorter than its diff:
```python
import functools

import jax
import jax.numpy as jnp
from jax import lax
from jax.experimental import pallas as pl
from jax.experimental.pallas import tpu as pltpu
from jax.sharding import PartitionSpec as P

HEAD_DIM = 128
LOG2E = 1.4426950408889634
NEG = -1e30


def dot_nt(a, b):
    return lax.dot_general(a, b, (((1,), (1,)), ((), ())), preferred_element_type=jnp.float32)


def dot_nn(a, b):
    return lax.dot_general(a, b, (((1,), (0,)), ((), ())), preferred_element_type=jnp.float32)


def dot_tn(a, b):
    return lax.dot_general(a, b, (((0,), (0,)), ((), ())), preferred_element_type=jnp.float32)


def fill_bias(bias, lengths_ref, counts_ref, me, rows, n_groups, per_group):
    length = lengths_ref[me]
    key_slot = lax.broadcasted_iota(jnp.int32, (rows, rows), 0)
    query_slot = lax.broadcasted_iota(jnp.int32, (rows, rows), 1)
    raw = (key_slot <= query_slot) & (key_slot < length)
    bias[0:rows, :] = jnp.where(raw, 0.0, NEG)
    slot = lax.broadcasted_iota(jnp.int32, (per_group, rows), 0)

    def one(group, carry):
        count = jnp.where(group < me, counts_ref[group], 0)
        at = pl.multiple_of(rows + group * per_group, per_group)
        bias[pl.ds(at, per_group), :] = jnp.where(slot < count, 0.0, NEG)
        return carry

    lax.fori_loop(0, n_groups, one, 0)


def attend(q, k, v, g, bk, bv, bias):
    rows = q.shape[0]
    scale = HEAD_DIM**-0.5
    keys = jnp.concatenate([k, bk], axis=0)
    vals = jnp.concatenate([v, bv], axis=0)
    scores = dot_nt(keys, q) * (scale * LOG2E) + bias[...]
    top = jnp.max(scores, axis=0, keepdims=True)
    expo = jnp.exp2(scores - top)
    total = jnp.sum(expo, axis=0, keepdims=True)
    probs = expo * (1.0 / total)
    low = probs.astype(jnp.bfloat16)
    dprobs = dot_nt(vals, g)
    delta = jnp.sum(low.astype(jnp.float32) * dprobs, axis=0, keepdims=True)
    dscores = (probs * (dprobs - delta)).astype(jnp.bfloat16)
    dq = (dot_tn(keys, dscores) * scale).T.astype(jnp.bfloat16)
    dkeys = (dot_nn(dscores, q) * scale).astype(jnp.bfloat16)
    dvals = dot_nn(low, g).astype(jnp.bfloat16)
    return dq, dkeys[:rows], dvals[:rows], dkeys[rows:], dvals[rows:]


class Grid:
    def __init__(self, n):
        self.C = 2
        chips = n // 2
        self.X = 1
        while self.X * self.X * 4 <= chips:
            self.X *= 2
        self.Z = chips // self.X
        self.me = lax.axis_index("ctx")
        self.c = lax.rem(self.me, 2)
        self.x = lax.rem(self.me // 2, self.X)
        self.z = self.me // (2 * self.X)
        self.up, self.down = self.me + 2 * self.X, self.me - 2 * self.X
        self.partner = self.me + 1 - 2 * self.c

    def at(self, z, x, c):
        return (z * self.X + x) * 2 + c

    def greet(self):
        barrier = pltpu.get_barrier_semaphore()

        def hello(ctx):
            pl.semaphore_signal(
                barrier, inc=1, device_id={"ctx": ctx}, device_id_type=pl.DeviceIdType.MESH
            )

        hello(self.partner)
        for dx in range(1, self.X):
            hello(self.at(self.z, lax.rem(self.x + dx, self.X), self.c))
        pl.when(self.z < self.Z - 1)(lambda: hello(self.up))
        pl.when(self.z > 0)(lambda: hello(self.down))
        ends = jnp.where(self.z > 0, 1, 0) + jnp.where(self.z < self.Z - 1, 1, 0)
        return barrier, self.X + ends


def remote(src, dst, send, recv, ctx, head=None):
    where = {"ctx": ctx} if head is None else {"ctx": ctx, "head": head}
    return pltpu.make_async_remote_copy(
        src_ref=src, dst_ref=dst, send_sem=send, recv_sem=recv,
        device_id=where, device_id_type=pl.DeviceIdType.MESH,
    )


class Spread:
    def __init__(self, grid, buf, sems, w, both_ways, cores):
        self.grid, self.buf, self.w = grid, buf, w
        self.recv, self.z_send, self.x_send, self.c_send = sems
        self.both_ways, self.cores = both_ways, cores

    def copy(self, i, send, ctx):
        block = self.buf.at[self.w, i]
        return remote(block, block, send, self.recv.at[self.w, i], ctx)

    def arrived(self, i):
        self.along_core(i).wait_recv()

    def along_core(self, i):
        return self.copy(i, self.c_send.at[self.w, i], self.grid.partner)

    def onward(self, zb, upward, downward, act):
        grid, w = self.grid, self.w
        i = grid.at(zb, grid.x, grid.c)
        if upward:
            up = self.copy(i, self.z_send.at[w, i, 0], grid.up)
            pl.when(grid.z < grid.Z - 1)(lambda: act(up))
        if downward:
            down = self.copy(i, self.z_send.at[w, i, 1], grid.down)
            pl.when(grid.z > 0)(lambda: act(down))
        for dx in range(1, grid.X):
            there = grid.at(grid.z, lax.rem(grid.x + dx, grid.X), grid.c)
            act(self.copy(i, self.x_send.at[w, i, dx - 1], there))
        if self.cores:
            act(self.along_core(i))

    def column(self, s, act, wait):
        grid = self.grid

        def there(zb, upward):
            if wait:
                self.arrived(grid.at(zb, grid.x, grid.c))
            self.onward(zb, upward, not upward, act)

        pl.when(grid.z - s >= 0)(lambda: there(grid.z - s, True))
        if self.both_ways:
            pl.when(grid.z + s < grid.Z)(lambda: there(grid.z + s, False))

    def cross(self, s, act, wait):
        grid = self.grid

        def row(zb):
            for dx in range(1, grid.X):
                i = grid.at(zb, lax.rem(grid.x + dx, grid.X), grid.c)
                if wait:
                    self.arrived(i)
                if self.cores:
                    act(self.along_core(i))

        if s == 0:
            row(grid.z)
            return
        pl.when(grid.z - s >= 0)(lambda: row(grid.z - s))
        if self.both_ways:
            pl.when(grid.z + s < grid.Z)(lambda: row(grid.z + s))

    def own(self):
        self.onward(self.grid.z, True, self.both_ways, lambda d: d.start())

    def step(self, s):
        self.column(s, lambda d: d.start(), True)
        self.cross(s - 1, lambda d: d.start(), True)

    def finish(self):
        grid = self.grid
        self.cross(grid.Z - 1, lambda d: d.start(), True)
        if not self.cores:
            return

        def last(zb):
            for xb in range(grid.X):
                self.arrived(grid.at(zb, xb, 1 - grid.c))

        for zb in range(grid.Z):
            pl.when((zb <= grid.z) | self.both_ways)(functools.partial(last, zb))

    def drain(self):
        def sent(d):
            d.wait_send()

        self.onward(self.grid.z, True, self.both_ways, sent)
        for s in range(1, self.grid.Z):
            self.column(s, sent, False)
        if self.cores:
            for s in range(self.grid.Z):
                self.cross(s, sent, False)


class Reduce:
    def __init__(self, grid, w, terms, core_in, x_out, x_in, z_out, z_in, acc, sems):
        self.grid, self.w, self.terms, self.core_in = grid, w, terms, core_in
        self.x_out, self.x_in, self.z_out, self.z_in, self.acc = x_out, x_in, z_out, z_in, acc
        self.core_sem, self.x_sem, self.z_sem = sems

    def to_core(self, zb, xb):
        grid, w = self.grid, self.w
        j = zb * grid.X + xb
        return remote(
            self.terms.at[w, grid.at(zb, xb, 1 - grid.c)], self.core_in.at[j, w],
            self.core_sem.at[0, w, j], self.core_sem.at[1, w, j], grid.partner,
        )

    def to_x(self, zb, dx):
        grid, w, d = self.grid, self.w, dx - 1
        return remote(
            self.x_out.at[zb, d, w], self.x_in.at[zb, d, w],
            self.x_sem.at[0, w, zb, d], self.x_sem.at[1, w, zb, d],
            grid.at(grid.z, lax.rem(grid.x + dx, grid.X), grid.c),
        )

    def to_z(self, zb):
        w = self.w
        return remote(
            self.z_out.at[zb, w], self.z_in.at[zb, w],
            self.z_sem.at[0, w, zb], self.z_sem.at[1, w, zb], self.grid.down,
        )

    def each_row(self, act):
        for zb in range(self.grid.Z):
            pl.when(zb <= self.grid.z)(functools.partial(act, zb))

    def start(self):
        def core_row(zb):
            for dx in range(self.grid.X):
                self.to_core(zb, lax.rem(self.grid.x + dx, self.grid.X)).start()

        self.each_row(core_row)

    def x_row(self, zb):
        grid, w = self.grid, self.w

        def act():
            for dx in list(range(1, grid.X)) + [0]:
                xb = lax.rem(grid.x + dx, grid.X)
                self.to_core(zb, xb).wait_recv()
                mine = self.terms[w, grid.at(zb, xb, grid.c)].astype(jnp.float32)
                total = mine + self.core_in[zb * grid.X + xb, w].astype(jnp.float32)
                if dx == 0:
                    self.acc[zb, w] = total
                else:
                    self.x_out[zb, dx - 1, w] = total.astype(jnp.bfloat16)
                    self.to_x(zb, dx).start()

        pl.when(zb <= grid.z)(act)

    def z_rows(self, grads):
        grid, w, acc = self.grid, self.w, self.acc

        def z_row(zb):
            total = acc[zb, w]
            for dx in range(1, grid.X):
                self.to_x(zb, dx).wait_recv()
                total = total + self.x_in[zb, dx - 1, w].astype(jnp.float32)
            acc[zb, w] = total

            @pl.when(grid.z < grid.Z - 1)
            def _():
                self.to_z(zb).wait_recv()
                acc[zb, w] = acc[zb, w] + self.z_in[zb, w].astype(jnp.float32)

            @pl.when(zb < grid.z)
            def _():
                self.z_out[zb, w] = acc[zb, w].astype(jnp.bfloat16)
                self.to_z(zb).start()

            @pl.when(zb == grid.z)
            def _():
                grads[w, grid.me] = acc[zb, w].astype(jnp.bfloat16)

        self.each_row(z_row)

    def drain(self):
        grid = self.grid

        def sent_row(zb):
            for dx in range(grid.X):
                self.to_core(zb, lax.rem(grid.x + dx, grid.X)).wait_send()
            for dx in range(1, grid.X):
                self.to_x(zb, dx).wait_send()
            pl.when(zb < grid.z)(lambda: self.to_z(zb).wait_send())

        self.each_row(sent_row)


def whole_kernel(
    n, n_heads, waves, lengths_ref, counts_ref, q_ref, k_ref, v_ref, g_ref, bk_ref, bv_ref,
    wk_ref, wv_ref,
    dq_ref, dk_ref, dv_ref, dbk_ref, dbv_ref, hidden_ref,
    bias, beacons, terms, core_in, x_out, x_in, z_out, z_in, acc, grads, weights, part, h_out, h_in,
    a_recv, a_z, a_x, a_c, d_recv, d_z, d_x, d_c, core_sem, x_sem, z_sem, w_sem, h_send, h_recv,
):
    grid = Grid(n)
    Z, X, z, c, me = grid.Z, grid.X, grid.z, grid.c, grid.me
    head = lax.axis_index("head")
    chips, per_head = n // 2, n // 2 // n_heads
    chip = me // 2
    to_head = chip // per_head
    per_group, width = bk_ref.shape
    rows = q_ref.shape[0]
    half = width // waves
    row = X * 2

    barrier, count = grid.greet()

    def source(j):
        return (head * per_head + j // n_heads) * 2 + c, lax.rem(j, n_heads)

    def hello(j, carry):
        src_c, src_h = source(j)

        @pl.when((src_c != me) | (src_h != head))
        def _():
            pl.semaphore_signal(
                barrier, inc=1, device_id={"ctx": src_c, "head": src_h},
                device_id_type=pl.DeviceIdType.MESH,
            )

        return carry

    lax.fori_loop(0, chips, hello, 0)
    for w in range(waves):
        beacons[w, me, :, 0:half] = bk_ref[:, w * half : (w + 1) * half]
        beacons[w, me, :, half : 2 * half] = bv_ref[:, w * half : (w + 1) * half]
    for zb in range(1, Z):

        def clear(zb=zb):
            zeros = jnp.zeros((row,) + beacons.shape[2:], beacons.dtype)
            for w in range(waves):
                beacons[w, zb * row : (zb + 1) * row] = zeros

        pl.when(zb > z)(clear)
    pl.semaphore_wait(barrier, count + chips - jnp.where(to_head == head, 1, 0))

    a_sems, d_sems = (a_recv, a_z, a_x, a_c), (d_recv, d_z, d_x, d_c)
    first = [Spread(grid, beacons, a_sems, w, False, True) for w in range(waves)]
    after = [Spread(grid, grads, d_sems, w, True, False) for w in range(waves)]
    sums = [
        Reduce(grid, w, terms, core_in, x_out, x_in, z_out, z_in, acc, (core_sem, x_sem, z_sem))
        for w in range(waves)
    ]
    first[0].own()
    weights[c, 0] = wk_ref[...]
    weights[c, 1] = wv_ref[...]
    fill_bias(bias, lengths_ref, counts_ref, me, rows, n, per_group)
    valid = lax.broadcasted_iota(jnp.int32, (rows, HEAD_DIM), 0) < lengths_ref[me]
    for s in range(1, Z):
        first[0].step(s)
        if s == 1:
            for w in range(1, waves):
                first[w].own()
    first[0].finish()
    to_partner = remote(
        weights.at[c], weights.at[c], w_sem.at[0], w_sem.at[1], grid.partner
    )
    to_partner.start()

    def one_head(w, slot):
        at = w * half + slot * HEAD_DIM
        cols, left = slice(at, at + HEAD_DIM), slot * HEAD_DIM
        right = half + left
        g = jnp.where(valid, g_ref[:, cols], jnp.zeros((rows, HEAD_DIM), jnp.bfloat16))
        bk = beacons[w, :, :, left : left + HEAD_DIM].reshape(n * per_group, HEAD_DIM)
        bv = beacons[w, :, :, right : right + HEAD_DIM].reshape(n * per_group, HEAD_DIM)
        dq, dk, dv, dkb, dvb = attend(q_ref[:, cols], k_ref[:, cols], v_ref[:, cols], g, bk, bv, bias)
        dq_ref[:, cols] = dq
        dk_ref[:, cols] = dk
        dv_ref[:, cols] = dv
        terms[w, :, :, left : left + HEAD_DIM] = dkb.reshape(n, per_group, HEAD_DIM)
        terms[w, :, :, right : right + HEAD_DIM] = dvb.reshape(n, per_group, HEAD_DIM)

    per_wave = half // HEAD_DIM
    for w in range(waves):
        between = []
        for s in range(1, Z):
            if w + 1 < waves:
                between.append(functools.partial(first[w + 1].step, s))
        for zb in range(Z):
            if w > 0:
                between.append(functools.partial(sums[w - 1].x_row, zb))
        for slot in range(per_wave):
            one_head(w, slot)
            for act in between[slot * len(between) // per_wave : (slot + 1) * len(between) // per_wave]:
                act()
        sums[w].start()
        if w + 1 < waves:
            first[w + 1].finish()

    top = z == Z - 1
    for w in range(waves - 1):
        pl.when(top)(functools.partial(sums[w].z_rows, grads))
    for zb in range(Z):
        sums[-1].x_row(zb)
    for w in range(waves):
        if w < waves - 1:
            pl.when(jnp.logical_not(top))(functools.partial(sums[w].z_rows, grads))
        else:
            sums[w].z_rows(grads)
        after[w].own()
        dbk_ref[:, w * half : (w + 1) * half] = grads[w, me, :, 0:half]
        dbv_ref[:, w * half : (w + 1) * half] = grads[w, me, :, half : 2 * half]
    for s in range(1, Z):
        for w in range(waves):
            after[w].step(s)

    cols = wk_ref.shape[0]
    my_slot = (chip - to_head * per_head) * n_heads + head
    to_partner.wait()

    def to_owner(b):
        return remote(
            h_out.at[b], h_in.at[my_slot], h_send.at[b], h_recv.at[my_slot], b * 2 + c, to_head
        )

    for w in range(waves):
        after[w].finish()
        span = slice(w * half, (w + 1) * half)
        for zb in range(Z):
            got = [grads[w, (zb * X + xb) * 2 + c] for xb in range(X)]
            block = jnp.concatenate(got, axis=0)
            for core in range(2):
                here = slice(core * cols, (core + 1) * cols)
                total = dot_nt(block[:, :half], weights[core, 0, :, span])
                total = total + dot_nt(block[:, half:], weights[core, 1, :, span])
                total = total.reshape(X, per_group, cols)
                if w > 0:
                    total = total + part[zb * X : (zb + 1) * X, :, here]
                if w < waves - 1:
                    part[zb * X : (zb + 1) * X, :, here] = total
                else:
                    h_out[zb * X : (zb + 1) * X, :, here] = total.astype(jnp.bfloat16)
            if w < waves - 1:
                continue
            for xb in range(X):
                b = zb * X + xb
                stays = (b == chip) & (to_head == head)

                @pl.when(stays)
                def _(b=b):
                    h_in[my_slot] = h_out[b]

                @pl.when(jnp.logical_not(stays))
                def _(b=b):
                    to_owner(b).start()

    def landed(j, carry):
        src_c, src_h = source(j)

        @pl.when((src_c != me) | (src_h != head))
        def _():
            remote(h_out.at[0], h_in.at[j], h_send.at[0], h_recv.at[j], me, head).wait_recv()

        return carry

    lax.fori_loop(0, chips, landed, 0)
    for j in range(per_head):
        total = h_in[j * n_heads].astype(jnp.float32)
        for h in range(1, n_heads):
            total = total + h_in[j * n_heads + h].astype(jnp.float32)
        hidden_ref[:, j * 2 * cols : (j + 1) * 2 * cols] = total.astype(jnp.bfloat16)

    for w in range(waves):
        first[w].drain()
        sums[w].drain()
        after[w].drain()

    def sent(b, carry):
        pl.when((b != chip) | (to_head != head))(lambda: to_owner(b).wait_send())
        return carry

    lax.fori_loop(0, chips, sent, 0)


def per_device(
    n_heads,
    queries,
    keys,
    values,
    dout,
    beacon_keys,
    beacon_values,
    beacon_key_weight,
    beacon_value_weight,
    lengths,
    counts,
):
    n = lengths.shape[0]
    rows, width = queries.shape
    per_group = beacon_keys.shape[0]
    cols = beacon_key_weight.shape[0]
    waves = 2 if (width // HEAD_DIM) % 2 == 0 else 1
    chips = n // 2
    X = 1
    while X * X * 4 <= chips:
        X *= 2
    Z, others = chips // X, max(X - 1, 1)
    low, f32, dma = jnp.bfloat16, jnp.float32, pltpu.SemaphoreType.DMA
    block = (per_group, 2 * width // waves)
    parts = (waves,) + block
    spread = [dma((waves, n)), dma((waves, n, 2)), dma((waves, n, others)), dma((waves, n))]
    raw = jax.ShapeDtypeStruct((rows, width), low)
    beacon = jax.ShapeDtypeStruct((per_group, width), low)
    vmem = pl.BlockSpec(memory_space=pltpu.VMEM)
    smem = pl.BlockSpec(memory_space=pltpu.SMEM)
    return pl.pallas_call(
        functools.partial(whole_kernel, n, n_heads, waves),
        out_shape=(
            raw, raw, raw, beacon, beacon,
            jax.ShapeDtypeStruct((per_group, cols * (n // n_heads)), low),
        ),
        in_specs=[smem, smem] + [vmem] * 8,
        out_specs=(vmem,) * 6,
        scratch_shapes=[
            pltpu.VMEM((rows + n * per_group, rows), f32),
            pltpu.VMEM((waves, n) + block, low),
            pltpu.VMEM((waves, n) + block, low),
            pltpu.VMEM((chips,) + parts, low),
            pltpu.VMEM((Z, others) + parts, low),
            pltpu.VMEM((Z, others) + parts, low),
            pltpu.VMEM((Z,) + parts, low),
            pltpu.VMEM((Z,) + parts, low),
            pltpu.VMEM((Z,) + parts, f32),
            pltpu.VMEM((waves, n) + block, low),
            pltpu.VMEM((2, 2, cols, width), low),
            pltpu.VMEM((chips, per_group, 2 * cols), f32),
            pltpu.VMEM((chips, per_group, 2 * cols), low),
            pltpu.VMEM((chips, per_group, 2 * cols), low),
        ]
        + spread
        + spread
        + [
            dma((2, waves, chips)), dma((2, waves, Z, others)), dma((2, waves, Z)),
            dma((2,)), dma((chips,)), dma((chips,)),
        ],
        compiler_params=pltpu.CompilerParams(
            collective_id=0, has_side_effects=True, vmem_limit_bytes=56 * 1024 * 1024
        ),
    )(
        lengths, counts, queries, keys, values, dout, beacon_keys, beacon_values,
        beacon_key_weight, beacon_value_weight,
    )


def solution(mesh):
    spec = P("ctx", "head")
    return jax.shard_map(
        functools.partial(per_device, mesh.shape["head"]),
        mesh=mesh,
        in_specs=(spec,) * 8 + (P(), P()),
        out_specs=(spec,) * 6,
        check_vma=False,
    )
```

time: 206 us -> 85.6 us (0.42)
  waiting for transfers between devices: 159 us -> 0 us
  Pallas kernels: 9.98 us -> 78.3 us
  blocking collectives: 13.3 us -> 0 us
  between operations: 13.9 us -> 0.66 us
  other arithmetic: 3.06 us -> 0 us
  matrix products: 2.34 us -> 0 us
    all_gather x2 -> x0, waiting for transfers between devices: 88.7 us -> none  [the longest x1 46 us: per_device(): gathered = lax.all_gather(both, 'ctx', axis=0, tiled=True)]
    reduce_scatter x2 -> x0, waiting for transfers between devices: 69.9 us -> none  [the longest x1 60.5 us: per_device(): summed = lax.psum_scatter(terms, 'ctx', scatter_dimension=0, tiled=True)]
    pallas_call x1, Pallas kernels: 9.98 us -> 78.3 us  [per_device(): pl.pallas_call(functools.partial(whole_kernel, n, n_heads, waves), out_sh...]
    all_to_all x1 -> x0, blocking collectives: 13.3 us -> none  [per_device(): mine = lax.all_to_all(part, 'ctx', split_axis=0, concat_axis=1, tiled=True)]
    unnamed x18 -> x16, local copies, waits for them, and re-layouts: 0.05 us -> 5.94 us
    slice x2 -> x0, local copies, waits for them, and re-layouts: 3.34 us -> none  [the longest x1 2.68 us: per_device(): gathered[:, width:]]
    concatenate x2 -> x0, other arithmetic: 3.06 us -> none  [the longest x1 1.54 us: per_device(): both = jnp.concatenate([beacon_keys, beacon_values], axis=1)]
    dot_general x1 -> x0, matrix products: 2.34 us -> none  [dot_nt(): lax.dot_general(a, b, (((1,), (1,)), ((), ())), preferred_element_type=jn...]
  transfers between devices with their start and end apart: 4 -> 0, of which waited for: 4 -> 0; matrix products, arithmetic and copies ran while one was open for 0% -> 0% of each run, Pallas kernels for 0% -> 0%
where the time goes in v3:
time: 85.6 us; the launch traced here: 84.9 us
  Pallas kernels  78.3 us (91%)
  local copies, waits for them, and re-layouts  5.94 us (7%)
    pallas_call x1, Pallas kernels, per_device(): pl.pallas_call(functools.partial(whole_kernel, n, n_heads, waves), out_sh...  78.3 us
    unnamed x16, local copies, waits for them, and re-layouts  5.94 us

profile of v3, /device:TPU:0, one launch (start us, length us, event | category | flops | bytes accessed | tf_op | source)
XLA Modules:
  0.0 84.9 jit_solution(438121235846400434)
XLA Ops:
  0.6 78.3 %shard_map.145 = (bf16[256,1024]{1,0:T(8,128)(2,1)}, bf16[256,1024]{1,0:T(8,128)(2,1)}, bf16[256,1024]{1,0:T(8,128)(2,1)}, bf16[32,1024]{1,0:T(8,128)(2,1)}, bf1...) custom-call(s32[16]{0:T(128)} %lengths_ref.1, s32[16]{0:T(128)} %counts_ref.1, bf16[256,1024]{1,0:T(8,128)(2,1)} %q_ref.1, ...), custom_call_target="tpu_custom_call" | custom-call | tf_op jit(solution)/shard_map/pallas_call | solution.py:515
  79.0 0.0 copy-start.1
  79.0 1.9 %copy.22 = bf16[256,1024]{1,0:T(8,128)(2,1)} copy(bf16[256,1024]{1,0:T(8,128)(2,1)} %get-tuple-element.12) | data formatting | bytes 1048576
  80.9 0.0 copy-done.1
  80.9 0.0 copy-start
  80.9 0.8 copy.23
  81.7 0.4 copy-done
  82.2 0.0 copy-start.4
  82.2 0.0 copy-start.3
  82.2 0.8 copy.24
  83.0 0.1 copy-done.4
  83.0 0.0 copy-start.2
  83.0 0.6 copy.25
  83.7 0.0 copy-done.3
  83.7 0.6 copy.26
  84.3 0.0 copy-done.2
  84.3 0.7 copy.27
Async XLA Ops:
  79.0 1.9 %copy-start.1 = (bf16[256,1024]{1,0:T(8,128)(2,1)S(1)}, bf16[256,1024]{1,0:T(8,128)(2,1)}, u32[]{:S(2)}) copy-start(bf16[256,1024]{1,0:T(8,128)(2,1)} %get-tuple-element.13) | copy-start | bytes 1572868
  80.9 1.2 %copy-start = (bf16[256,1024]{1,0:T(8,128)(2,1)S(1)}, bf16[256,1024]{1,0:T(8,128)(2,1)}, u32[]{:S(2)}) copy-start(bf16[256,1024]{1,0:T(8,128)(2,1)} %get-tuple-element.14) | copy-start | bytes 1572868
  82.2 0.9 %copy-start.4 = (bf16[32,1024]{1,0:T(8,128)(2,1)S(1)}, bf16[32,1024]{1,0:T(8,128)(2,1)}, u32[]{:S(2)}) copy-start(bf16[32,1024]{1,0:T(8,128)(2,1)} %get-tuple-element.15) | copy-start | bytes 196612
  82.2 1.5 %copy-start.3 = (bf16[32,1024]{1,0:T(8,128)(2,1)S(1)}, bf16[32,1024]{1,0:T(8,128)(2,1)}, u32[]{:S(2)}) copy-start(bf16[32,1024]{1,0:T(8,128)(2,1)} %get-tuple-element.16) | copy-start | bytes 196612
  83.0 1.3 %copy-start.2 = (bf16[32,2048]{1,0:T(8,128)(2,1)S(1)}, bf16[32,2048]{1,0:T(8,128)(2,1)}, u32[]{:S(2)}) copy-start(bf16[32,2048]{1,0:T(8,128)(2,1)} %get-tuple-element.17) | copy-start | bytes 393220

commit v4 on v3

--- a/solution.py
+++ b/solution.py
@@ -79,21 +79,22 @@
     def at(self, z, x, c):
         return (z * self.X + x) * 2 + c
 
-    def greet(self):
+    def greet(self, n_heads):
         barrier = pltpu.get_barrier_semaphore()
 
-        def hello(ctx):
+        def hello(where):
             pl.semaphore_signal(
-                barrier, inc=1, device_id={"ctx": ctx}, device_id_type=pl.DeviceIdType.MESH
+                barrier, inc=1, device_id=where, device_id_type=pl.DeviceIdType.MESH
             )
 
-        hello(self.partner)
-        for dx in range(1, self.X):
-            hello(self.at(self.z, lax.rem(self.x + dx, self.X), self.c))
-        pl.when(self.z < self.Z - 1)(lambda: hello(self.up))
-        pl.when(self.z > 0)(lambda: hello(self.down))
-        ends = jnp.where(self.z > 0, 1, 0) + jnp.where(self.z < self.Z - 1, 1, 0)
-        return barrier, self.X + ends
+        chips = self.X * self.Z
+        hello({"ctx": self.partner})
+        for k in range(1, chips):
+            hello({"ctx": lax.rem(self.me + 2 * k, 2 * chips)})
+        head = lax.axis_index("head")
+        for k in range(1, n_heads):
+            hello({"head": lax.rem(head + k, n_heads)})
+        return barrier, chips + n_heads - 1
 
 
 def remote(src, dst, send, recv, ctx, head=None):
@@ -297,38 +298,20 @@
     n, n_heads, waves, lengths_ref, counts_ref, q_ref, k_ref, v_ref, g_ref, bk_ref, bv_ref,
     wk_ref, wv_ref,
     dq_ref, dk_ref, dv_ref, dbk_ref, dbv_ref, hidden_ref,
-    bias, beacons, terms, core_in, x_out, x_in, z_out, z_in, acc, grads, weights, part, h_out, h_in,
-    a_recv, a_z, a_x, a_c, d_recv, d_z, d_x, d_c, core_sem, x_sem, z_sem, w_sem, h_send, h_recv,
+    bias, beacons, terms, core_in, x_out, x_in, z_out, z_in, acc, grads, weights, part, h_out, h_in, y_in,
+    a_recv, a_z, a_x, a_c, d_recv, d_z, d_x, d_c, core_sem, x_sem, z_sem, w_sem, h_send, h_recv, y_send, y_recv,
 ):
     grid = Grid(n)
     Z, X, z, c, me = grid.Z, grid.X, grid.z, grid.c, grid.me
     head = lax.axis_index("head")
     chips, per_head = n // 2, n // 2 // n_heads
     chip = me // 2
-    to_head = chip // per_head
     per_group, width = bk_ref.shape
     rows = q_ref.shape[0]
     half = width // waves
     row = X * 2
 
-    barrier, count = grid.greet()
-
-    def source(j):
-        return (head * per_head + j // n_heads) * 2 + c, lax.rem(j, n_heads)
-
-    def hello(j, carry):
-        src_c, src_h = source(j)
-
-        @pl.when((src_c != me) | (src_h != head))
-        def _():
-            pl.semaphore_signal(
-                barrier, inc=1, device_id={"ctx": src_c, "head": src_h},
-                device_id_type=pl.DeviceIdType.MESH,
-            )
-
-        return carry
-
-    lax.fori_loop(0, chips, hello, 0)
+    barrier, count = grid.greet(n_heads)
     for w in range(waves):
         beacons[w, me, :, 0:half] = bk_ref[:, w * half : (w + 1) * half]
         beacons[w, me, :, half : 2 * half] = bv_ref[:, w * half : (w + 1) * half]
@@ -340,7 +323,7 @@
                 beacons[w, zb * row : (zb + 1) * row] = zeros
 
         pl.when(zb > z)(clear)
-    pl.semaphore_wait(barrier, count + chips - jnp.where(to_head == head, 1, 0))
+    pl.semaphore_wait(barrier, count)
 
     a_sems, d_sems = (a_recv, a_z, a_x, a_c), (d_recv, d_z, d_x, d_c)
     first = [Spread(grid, beacons, a_sems, w, False, True) for w in range(waves)]
@@ -350,8 +333,10 @@
         for w in range(waves)
     ]
     first[0].own()
-    weights[c, 0] = wk_ref[...]
-    weights[c, 1] = wv_ref[...]
+    for w in range(waves):
+        span = slice(w * half, (w + 1) * half)
+        weights[c, w, 0:half, :] = wk_ref[:, span].T
+        weights[c, w, half : 2 * half, :] = wv_ref[:, span].T
     fill_bias(bias, lengths_ref, counts_ref, me, rows, n, per_group)
     valid = lax.broadcasted_iota(jnp.int32, (rows, HEAD_DIM), 0) < lengths_ref[me]
     for s in range(1, Z):
@@ -414,59 +399,46 @@
             after[w].step(s)
 
     cols = wk_ref.shape[0]
-    my_slot = (chip - to_head * per_head) * n_heads + head
     to_partner.wait()
-
-    def to_owner(b):
-        return remote(
-            h_out.at[b], h_in.at[my_slot], h_send.at[b], h_recv.at[my_slot], b * 2 + c, to_head
-        )
-
     for w in range(waves):
         after[w].finish()
-        span = slice(w * half, (w + 1) * half)
-        for zb in range(Z):
-            got = [grads[w, (zb * X + xb) * 2 + c] for xb in range(X)]
-            block = jnp.concatenate(got, axis=0)
-            for core in range(2):
-                here = slice(core * cols, (core + 1) * cols)
-                total = dot_nt(block[:, :half], weights[core, 0, :, span])
-                total = total + dot_nt(block[:, half:], weights[core, 1, :, span])
-                total = total.reshape(X, per_group, cols)
-                if w > 0:
-                    total = total + part[zb * X : (zb + 1) * X, :, here]
-                if w < waves - 1:
-                    part[zb * X : (zb + 1) * X, :, here] = total
-                else:
-                    h_out[zb * X : (zb + 1) * X, :, here] = total.astype(jnp.bfloat16)
+        block = jnp.concatenate([grads[w, b * 2 + c] for b in range(chips)], axis=0)
+        for core in range(2):
+            here = slice(core * cols, (core + 1) * cols)
+            total = dot_nn(block, weights[core, w]).reshape(chips, per_group, cols)
+            if w > 0:
+                total = total + part[:, :, here]
             if w < waves - 1:
-                continue
-            for xb in range(X):
-                b = zb * X + xb
-                stays = (b == chip) & (to_head == head)
-
-                @pl.when(stays)
-                def _(b=b):
-                    h_in[my_slot] = h_out[b]
-
-                @pl.when(jnp.logical_not(stays))
-                def _(b=b):
-                    to_owner(b).start()
-
-    def landed(j, carry):
-        src_c, src_h = source(j)
-
-        @pl.when((src_c != me) | (src_h != head))
-        def _():
-            remote(h_out.at[0], h_in.at[j], h_send.at[0], h_recv.at[j], me, head).wait_recv()
-
-        return carry
-
-    lax.fori_loop(0, chips, landed, 0)
+                part[:, :, here] = total
+            else:
+                h_out[:, :, here] = total.astype(jnp.bfloat16)
+
+    def to_group(b):
+        return remote(h_out.at[b], h_in.at[chip], h_send.at[b], h_recv.at[chip], b * 2 + c)
+
+    def to_head(b, owner):
+        slot = b - owner * per_head
+        return remote(
+            h_in.at[b], y_in.at[slot, head], y_send.at[b], y_recv.at[slot, head], me, owner
+        )
+
+    for k in range(1, chips):
+        to_group(lax.rem(chip + k, chips)).start()
+    h_in[chip] = h_out[chip]
+    for k in range(chips):
+        b = lax.rem(chip + k, chips)
+        if k > 0:
+            remote(h_out.at[0], h_in.at[b], h_send.at[0], h_recv.at[b], me).wait_recv()
+        owner = b // per_head
+        pl.when(owner != head)(lambda b=b, owner=owner: to_head(b, owner).start())
     for j in range(per_head):
-        total = h_in[j * n_heads].astype(jnp.float32)
-        for h in range(1, n_heads):
-            total = total + h_in[j * n_heads + h].astype(jnp.float32)
+        total = h_in[head * per_head + j].astype(jnp.float32)
+        for k in range(1, n_heads):
+            other = lax.rem(head + k, n_heads)
+            remote(
+                h_in.at[0], y_in.at[j, other], y_send.at[0], y_recv.at[j, other], me, other
+            ).wait_recv()
+            total = total + y_in[j, other].astype(jnp.float32)
         hidden_ref[:, j * 2 * cols : (j + 1) * 2 * cols] = total.astype(jnp.bfloat16)
 
     for w in range(waves):
@@ -474,11 +446,12 @@
         sums[w].drain()
         after[w].drain()
 
-    def sent(b, carry):
-        pl.when((b != chip) | (to_head != head))(lambda: to_owner(b).wait_send())
-        return carry
-
-    lax.fori_loop(0, chips, sent, 0)
+    for k in range(chips):
+        b = lax.rem(chip + k, chips)
+        if k > 0:
+            to_group(b).wait_send()
+        owner = b // per_head
+        pl.when(owner != head)(lambda b=b, owner=owner: to_head(b, owner).wait_send())
 
 
 def per_device(
@@ -531,16 +504,17 @@
             pltpu.VMEM((Z,) + parts, low),
             pltpu.VMEM((Z,) + parts, f32),
             pltpu.VMEM((waves, n) + block, low),
-            pltpu.VMEM((2, 2, cols, width), low),
+            pltpu.VMEM((2, waves, 2 * width // waves, cols), low),
             pltpu.VMEM((chips, per_group, 2 * cols), f32),
             pltpu.VMEM((chips, per_group, 2 * cols), low),
             pltpu.VMEM((chips, per_group, 2 * cols), low),
+            pltpu.VMEM((chips // n_heads, n_heads, per_group, 2 * cols), low),
         ]
         + spread
         + spread
         + [
             dma((2, waves, chips)), dma((2, waves, Z, others)), dma((2, waves, Z)),
-            dma((2,)), dma((chips,)), dma((chips,)),
+            dma((2,)), dma((chips,)), dma((chips,)), dma((chips,)), dma((chips // n_heads, n_heads)),
         ],
         compiler_params=pltpu.CompilerParams(
             collective_id=0, has_side_effects=True, vmem_limit_bytes=56 * 1024 * 1024

time: 85.6 us -> 88.7 us (1.036); the launches traced: 84.9 us -> 87.1 us
  Pallas kernels: 78.3 us -> 80.5 us
    pallas_call x1, Pallas kernels: 78.3 us -> 80.5 us  [per_device(): pl.pallas_call(functools.partial(whole_kernel, n, n_heads, waves), out_sh...]
where the time goes in v4:
time: 88.7 us; the launch traced here: 87.1 us
  Pallas kernels  80.5 us (91%)
  local copies, waits for them, and re-layouts  5.94 us (7%)
    pallas_call x1, Pallas kernels, per_device(): pl.pallas_call(functools.partial(whole_kernel, n, n_heads, waves), out_sh...  80.5 us
    unnamed x16, local copies, waits for them, and re-layouts  5.94 us

profile of v4, /device:TPU:0, one launch (start us, length us, event | category | flops | bytes accessed | tf_op | source)
XLA Modules:
  0.0 87.1 jit_solution(7302995669801925244)
XLA Ops:
  0.6 80.5 %shard_map.145 = (bf16[256,1024]{1,0:T(8,128)(2,1)}, bf16[256,1024]{1,0:T(8,128)(2,1)}, bf16[256,1024]{1,0:T(8,128)(2,1)}, bf16[32,1024]{1,0:T(8,128)(2,1)}, bf1...) custom-call(s32[16]{0:T(128)} %lengths_ref.1, s32[16]{0:T(128)} %counts_ref.1, bf16[256,1024]{1,0:T(8,128)(2,1)} %q_ref.1, ...), custom_call_target="tpu_custom_call" | custom-call | tf_op jit(solution)/shard_map/pallas_call | solution.py:488
  81.1 0.0 copy-start.1
  81.2 1.9 %copy.22 = bf16[256,1024]{1,0:T(8,128)(2,1)} copy(bf16[256,1024]{1,0:T(8,128)(2,1)} %get-tuple-element.12) | data formatting | bytes 1048576
  83.1 0.0 copy-done.1
  83.1 0.0 copy-start
  83.1 0.8 copy.23
  83.9 0.4 copy-done
  84.3 0.0 copy-start.4
  84.3 0.0 copy-start.3
  84.3 0.8 copy.24
  85.1 0.1 copy-done.4
  85.2 0.0 copy-start.2
  85.2 0.6 copy.25
  85.8 0.0 copy-done.3
  85.8 0.6 copy.26
  86.4 0.0 copy-done.2
  86.4 0.7 copy.27
Async XLA Ops:
  81.1 1.9 %copy-start.1 = (bf16[256,1024]{1,0:T(8,128)(2,1)S(1)}, bf16[256,1024]{1,0:T(8,128)(2,1)}, u32[]{:S(2)}) copy-start(bf16[256,1024]{1,0:T(8,128)(2,1)} %get-tuple-element.13) | copy-start | bytes 1572868
  83.1 1.2 %copy-start = (bf16[256,1024]{1,0:T(8,128)(2,1)S(1)}, bf16[256,1024]{1,0:T(8,128)(2,1)}, u32[]{:S(2)}) copy-start(bf16[256,1024]{1,0:T(8,128)(2,1)} %get-tuple-element.14) | copy-start | bytes 1572868
  84.3 0.9 copy-start.4
  84.3 1.5 %copy-start.3 = (bf16[32,1024]{1,0:T(8,128)(2,1)S(1)}, bf16[32,1024]{1,0:T(8,128)(2,1)}, u32[]{:S(2)}) copy-start(bf16[32,1024]{1,0:T(8,128)(2,1)} %get-tuple-element.16) | copy-start | bytes 196612
  85.2 1.3 %copy-start.2 = (bf16[32,2048]{1,0:T(8,128)(2,1)S(1)}, bf16[32,2048]{1,0:T(8,128)(2,1)}, u32[]{:S(2)}) copy-start(bf16[32,2048]{1,0:T(8,128)(2,1)} %get-tuple-element.17) | copy-start | bytes 393220

commit v5 on v2

--- a/solution.py
+++ b/solution.py
@@ -90,7 +90,7 @@
         in_specs=[smem, smem] + [vmem] * 5,
         out_specs=(vmem,) * 4,
         scratch_shapes=[pltpu.VMEM((rows + slots, rows), jnp.float32)],
-        compiler_params=pltpu.CompilerParams(vmem_limit_bytes=48 * 1024 * 1024),
+        compiler_params=pltpu.CompilerParams(vmem_limit_bytes=60 * 1024 * 1024),
     )(lengths, counts, q, k, v, g, beacons)
 
 
@@ -264,13 +264,14 @@
         out_specs=vmem,
         scratch_shapes=spread_sems(n),
         compiler_params=pltpu.CompilerParams(
-            collective_id=0, has_side_effects=True, vmem_limit_bytes=48 * 1024 * 1024
+            collective_id=0, has_side_effects=True, vmem_limit_bytes=60 * 1024 * 1024
         ),
     )(bk, bv)
 
 
 def reduce_kernel(
-    n, n_heads, terms_ref, wk_ref, wv_ref, own_ref, hidden_ref,
+    n, n_heads, terms_ref, wk_hbm, wv_hbm, own_ref, hidden_ref,
+    wk_ref, wv_ref, w_sem,
     grads, core_in, x_out, x_in, z_out, z_in, acc, h_out, h_in,
     recv, z_send, x_send, c_send, core_sem, xr_sem, zr_sem, h_send, h_recv,
 ):
@@ -282,6 +283,13 @@
     width = wk_ref.shape[1]
     f32 = jnp.float32
 
+    own_rows = [
+        pltpu.make_async_copy(wk_hbm, wk_ref, w_sem.at[0]),
+        pltpu.make_async_copy(wv_hbm, wv_ref, w_sem.at[1]),
+    ]
+    for piece in own_rows:
+        piece.start()
+
     barrier, count = grid.greet()
 
     def hello(j, carry):
@@ -337,8 +345,6 @@
                 x_out[zb, dx - 1] = total.astype(jnp.bfloat16)
                 to_x(zb, dx).start()
 
-    each_row(x_row)
-
     def z_row(zb):
         total = acc[zb]
         for dx in range(1, X):
@@ -360,37 +366,44 @@
         def _():
             grads[me] = acc[zb].astype(jnp.bfloat16)
 
-    each_row(z_row)
+    def row_or_not(act, zb):
+        pl.when(zb <= z)(functools.partial(act, zb))
+
+    row_or_not(x_row, 0)
+    for zb in range(Z):
+        if zb + 1 < Z:
+            row_or_not(x_row, zb + 1)
+        row_or_not(z_row, zb)
     own_ref[...] = grads[me]
     drain = spread_blocks(grid, grads, recv, z_send, x_send, c_send, True)
 
     rows = own_ref.shape[0]
-    row = X * 2
     my_slot = (me - to_head * per_head) * n_heads + head
 
     def to_owner(b):
         return remote(h_out.at[b], h_in.at[my_slot], h_send.at[b], h_recv.at[my_slot], b, to_head)
 
-    for zb in range(Z):
-        block = grads[zb * row : (zb + 1) * row].reshape(row * rows, 2 * width)
-        part = dot_nt(block[:, :width], wk_ref[...]) + dot_nt(block[:, width:], wv_ref[...])
-        h_out[zb * row : (zb + 1) * row] = part.astype(jnp.bfloat16).reshape(row, rows, -1)
-
-        def send(j, carry, zb=zb):
-            b = zb * row + j
-            here = (b == me) & (to_head == head)
-
-            @pl.when(here)
-            def _():
-                h_in[my_slot] = h_out[b]
-
-            @pl.when(jnp.logical_not(here))
-            def _():
-                to_owner(b).start()
-
-            return carry
-
-        lax.fori_loop(0, row, send, 0)
+    for piece in own_rows:
+        piece.wait()
+    block = grads[...].reshape(n * rows, 2 * width)
+    part = dot_nt(block[:, :width], wk_ref[...]) + dot_nt(block[:, width:], wv_ref[...])
+    h_out[...] = part.astype(jnp.bfloat16).reshape(n, rows, -1)
+
+    def send(j, carry):
+        b = lax.rem(me + 1 + j, n)
+        here = (b == me) & (to_head == head)
+
+        @pl.when(here)
+        def _():
+            h_in[my_slot] = h_out[b]
+
+        @pl.when(jnp.logical_not(here))
+        def _():
+            to_owner(b).start()
+
+        return carry
+
+    lax.fori_loop(0, n, send, 0)
 
     def landed(j, carry):
         src_c, src_h = head * per_head + j // n_heads, lax.rem(j, n_heads)
@@ -443,9 +456,12 @@
             jax.ShapeDtypeStruct((rows, both), low),
             jax.ShapeDtypeStruct((rows, cols * (n // n_heads)), low),
         ),
-        in_specs=[vmem] * 3,
+        in_specs=[vmem, pl.BlockSpec(memory_space=pl.ANY), pl.BlockSpec(memory_space=pl.ANY)],
         out_specs=(vmem, vmem),
         scratch_shapes=[
+            pltpu.VMEM((cols, width), low),
+            pltpu.VMEM((cols, width), low),
+            dma((2,)),
             pltpu.VMEM((n, rows, both), low),
             pltpu.VMEM((Z * X, rows, both), low),
             pltpu.VMEM((Z, others, rows, both), low),
@@ -459,7 +475,7 @@
         + sems
         + [dma((2, Z * X)), dma((2, Z, others)), dma((2, Z)), dma((n,)), dma((n,))],
         compiler_params=pltpu.CompilerParams(
-            collective_id=1, has_side_effects=True, vmem_limit_bytes=48 * 1024 * 1024
+            collective_id=1, has_side_effects=True, vmem_limit_bytes=60 * 1024 * 1024
         ),
     )(terms, wk, wv)
 

time: 82.4 us -> 86.9 us (1.055)
  Pallas kernels: 75.8 us -> 81.5 us
  local copies, waits for them, and re-layouts: 4.46 us -> 3.1 us
    pallas_call x1, Pallas kernels: 56 us -> 58.2 us  [reduce_beacons(): pl.pallas_call(functools.partial(reduce_kernel, n, n_heads), out_shape=(j...]
    unnamed x23 -> x1, local copies, waits for them, and re-layouts: 3.8 us -> 1.57 us
    pallas_call x1, Pallas kernels: 9.43 us -> 11.6 us  [gather_beacons(): pl.pallas_call(functools.partial(gather_kernel, n), out_shape=jax.ShapeDt...]
    pallas_call x1, Pallas kernels: 10.4 us -> 11.7 us  [attention(): pl.pallas_call(functools.partial(attention_kernel, n_groups), out_shape=(...]
where the time goes in v5:
time: 86.9 us; the launch traced here: 85.3 us
  Pallas kernels  81.5 us (94%)
  local copies, waits for them, and re-layouts  3.1 us (4%)
    pallas_call x1, Pallas kernels, reduce_beacons(): pl.pallas_call(functools.partial(reduce_kernel, n, n_heads), out_shape=(j...  58.2 us
    pallas_call x1, Pallas kernels, attention(): pl.pallas_call(functools.partial(attention_kernel, n_groups), out_shape=(...  11.7 us
    pallas_call x1, Pallas kernels, gather_beacons(): pl.pallas_call(functools.partial(gather_kernel, n), out_shape=jax.ShapeDt...  11.6 us

profile of v5, /device:TPU:0, one launch (start us, length us, event | category | flops | bytes accessed | tf_op | source)
XLA Modules:
  0.0 85.3 jit_solution(11285001449049109294)
XLA Ops:
  0.6 11.6 %shard_map.145 = bf16[16,32,2048]{2,1,0:T(8,128)(2,1)} custom-call(bf16[32,1024]{1,0:T(8,128)(2,1)} %bk_ref.1, bf16[32,1024]{1,0:T(8,128)(2,1)} %bv_ref.1), custom_call_target="tpu_custom_call" | custom-call | tf_op jit(solution)/shard_map/pallas_call | solution.py:260
  12.3 11.7 %shard_map.146 = (bf16[256,1024]{1,0:T(8,128)(2,1)}, bf16[256,1024]{1,0:T(8,128)(2,1)}, bf16[256,1024]{1,0:T(8,128)(2,1)}, bf16[512,2048]{1,0:T(8,128)(2,1)}) custom-call(s32[16]{0:T(128)} %lengths_ref.1, s32[16]{0:T(128)} %counts_ref.1, bf16[256,1024]{1,0:T(8,128)(2,1)} %q_ref.1, bf16[256,1024]{1,0:T(8,128)(2,1)} %k_ref.1, bf16[256,1024]{1,0:T(8,128)(2,1)} %v_ref.1, ...), custom_call_target="tpu_custom_call" | custom-call | tf_op jit(solution)/shard_map/pallas_call | solution.py:87
  24.0 58.2 %shard_map.147 = (bf16[32,2048]{1,0:T(8,128)(2,1)}, bf16[32,2048]{1,0:T(8,128)(2,1)}) custom-call(bf16[16,32,2048]{2,1,0:T(8,128)(2,1)} %bitcast.3, bf16[256,1024]{1,0:T(8,128)(2,1)} %wk_hbm.1, bf16[256,1024]{1,0:T(8,128)(2,1)} %wv_hbm.1), custom_call_target="tpu_custom_call" | custom-call | tf_op jit(solution)/shard_map/pallas_call | solution.py:453
  82.2 1.5 %fusion = (bf16[32,1024]{1,0:T(8,128)(2,1)}, bf16[32,1024]{1,0:T(8,128)(2,1)}) fusion(bf16[32,2048]{1,0:T(8,128)(2,1)} %get-tuple-element.16), kind=kLoop, calls=%fused_computation | loop fusion | bytes 262144 | tf_op jit(solution)/shard_map/slice | solution.py:505
  83.7 1.6 %copy.17 = bf16[32,2048]{1,0:T(8,128)(2,1)} copy(bf16[32,2048]{1,0:T(8,128)(2,1)} %get-tuple-element.31) | data formatting | bytes 262144

commit v6 on v2

--- a/solution.py
+++ b/solution.py
@@ -90,7 +90,7 @@
         in_specs=[smem, smem] + [vmem] * 5,
         out_specs=(vmem,) * 4,
         scratch_shapes=[pltpu.VMEM((rows + slots, rows), jnp.float32)],
-        compiler_params=pltpu.CompilerParams(vmem_limit_bytes=48 * 1024 * 1024),
+        compiler_params=pltpu.CompilerParams(vmem_limit_bytes=40 * 1024 * 1024),
     )(lengths, counts, q, k, v, g, beacons)
 
 
@@ -264,7 +264,7 @@
         out_specs=vmem,
         scratch_shapes=spread_sems(n),
         compiler_params=pltpu.CompilerParams(
-            collective_id=0, has_side_effects=True, vmem_limit_bytes=48 * 1024 * 1024
+            collective_id=0, has_side_effects=True, vmem_limit_bytes=16 * 1024 * 1024
         ),
     )(bk, bv)
 
@@ -459,7 +459,7 @@
         + sems
         + [dma((2, Z * X)), dma((2, Z, others)), dma((2, Z)), dma((n,)), dma((n,))],
         compiler_params=pltpu.CompilerParams(
-            collective_id=1, has_side_effects=True, vmem_limit_bytes=48 * 1024 * 1024
+            collective_id=1, has_side_effects=True, vmem_limit_bytes=32 * 1024 * 1024
         ),
     )(terms, wk, wv)
 

time: 82.4 us -> 80 us (0.971)
  local copies, waits for them, and re-layouts: 4.46 us -> 3.14 us
  Pallas kernels: 75.8 us -> 74.7 us
    unnamed x23 -> x21, local copies, waits for them, and re-layouts: 3.8 us -> 2.48 us
    pallas_call x1, Pallas kernels: 10.4 us -> 9.33 us  [attention(): pl.pallas_call(functools.partial(attention_kernel, n_groups), out_shape=(...]
where the time goes in v6:
time: 80 us; the launch traced here: 78.6 us
  Pallas kernels  74.7 us (93%)
  local copies, waits for them, and re-layouts  3.14 us (4%)
    pallas_call x1, Pallas kernels, reduce_beacons(): pl.pallas_call(functools.partial(reduce_kernel, n, n_heads), out_shape=(j...  55.9 us
    pallas_call x1, Pallas kernels, gather_beacons(): pl.pallas_call(functools.partial(gather_kernel, n), out_shape=jax.ShapeDt...  9.43 us
    pallas_call x1, Pallas kernels, attention(): pl.pallas_call(functools.partial(attention_kernel, n_groups), out_shape=(...  9.33 us
    unnamed x21, local copies, waits for them, and re-layouts  2.48 us

profile of v6, /device:TPU:0, one launch (start us, length us, event | category | flops | bytes accessed | tf_op | source)
XLA Modules:
  0.0 78.6 jit_solution(4428957391518515854)
XLA Ops:
  0.6 0.0 copy-start.3
  0.6 0.0 copy-start.2
  0.7 0.0 copy-start.1
  0.7 0.0 copy-start.6
  0.7 0.9 %copy-done.6 = bf16[32,1024]{1,0:T(8,128)(2,1)S(1)} copy-done((bf16[32,1024]{1,0:T(8,128)(2,1)S(1)}, bf16[32,1024]{1,0:T(8,128)(2,1)}, u32[]{:S(2)}) %copy-start.6) | copy-done | bytes 65560
  1.6 0.0 copy-start.7
  1.6 0.8 %copy-done.7 = bf16[32,1024]{1,0:T(8,128)(2,1)S(1)} copy-done((bf16[32,1024]{1,0:T(8,128)(2,1)S(1)}, bf16[32,1024]{1,0:T(8,128)(2,1)}, u32[]{:S(2)}) %copy-start.7) | copy-done | bytes 65560
  2.5 0.0 copy-start
  2.5 0.0 copy-start.8
  2.5 0.0 copy-start.9
  2.5 9.4 %shard_map.145 = bf16[16,32,2048]{2,1,0:T(8,128)(2,1)S(1)} custom-call(bf16[32,1024]{1,0:T(8,128)(2,1)S(1)} %copy-done.6, bf16[32,1024]{1,0:T(8,128)(2,1)S(1)} %copy-done.7), custom_call_target="tpu_custom_call" | custom-call | tf_op jit(solution)/shard_map/pallas_call | solution.py:260
  11.9 0.0 copy-done.3
  11.9 0.0 copy-done.2
  11.9 0.0 copy-done.1
  11.9 0.0 copy-done
  11.9 0.0 copy-done.8
  12.0 0.0 copy-done.9
  12.0 0.0 copy-start.4
  12.0 0.0 copy-start.5
  12.0 9.3 %shard_map.146 = (bf16[256,1024]{1,0:T(8,128)(2,1)}, bf16[256,1024]{1,0:T(8,128)(2,1)}, bf16[256,1024]{1,0:T(8,128)(2,1)}, bf16[512,2048]{1,0:T(8,128)(2,1)S(1)}) custom-call(s32[16]{0:T(128)S(1)} %copy-done.8, s32[16]{0:T(128)S(1)} %copy-done.9, bf16[256,1024]{1,0:T(8,128)(2,1)S(1)} %copy-done, bf16[256,1024]{1,0:T(8,128)(2,1)S(1)} %copy-done.1, ...), custom_call_target="tpu_custom_call" | custom-call | tf_op jit(solution)/shard_map/pallas_call | solution.py:87
  21.3 0.0 copy-done.4
  21.3 0.0 copy-done.5
  21.3 55.9 %shard_map.147 = (bf16[32,2048]{1,0:T(8,128)(2,1)S(1)}, bf16[32,2048]{1,0:T(8,128)(2,1)S(1)}) custom-call(bf16[16,32,2048]{2,1,0:T(8,128)(2,1)S(1)} %bitcast.3, bf16[256,1024]{1,0:T(8,128)(2,1)S(1)} %copy-done.4, bf16[256,1024]{1,0:T(8,128)(2,1)S(1)} %copy-done.5), custom_call_target="tpu_custom_call" | custom-call | tf_op jit(solution)/shard_map/pallas_call | solution.py:440
  77.3 0.7 fusion
  77.9 0.7 copy.17
Async XLA Ops:
  0.6 11.3 %copy-start.3 = (bf16[256,1024]{1,0:T(8,128)(2,1)S(1)}, bf16[256,1024]{1,0:T(8,128)(2,1)}, u32[]{:S(2)}) copy-start(bf16[256,1024]{1,0:T(8,128)(2,1)} %g_ref.1) | copy-start | bytes 1572868
  0.6 11.3 %copy-start.2 = (bf16[256,1024]{1,0:T(8,128)(2,1)S(1)}, bf16[256,1024]{1,0:T(8,128)(2,1)}, u32[]{:S(2)}) copy-start(bf16[256,1024]{1,0:T(8,128)(2,1)} %v_ref.1) | copy-start | bytes 1572868
  0.7 11.3 %copy-start.1 = (bf16[256,1024]{1,0:T(8,128)(2,1)S(1)}, bf16[256,1024]{1,0:T(8,128)(2,1)}, u32[]{:S(2)}) copy-start(bf16[256,1024]{1,0:T(8,128)(2,1)} %k_ref.1) | copy-start | bytes 1572868
  0.7 1.0 %copy-start.6 = (bf16[32,1024]{1,0:T(8,128)(2,1)S(1)}, bf16[32,1024]{1,0:T(8,128)(2,1)}, u32[]{:S(2)}) copy-start(bf16[32,1024]{1,0:T(8,128)(2,1)} %bk_ref.1) | copy-start | bytes 196612
  1.6 0.8 %copy-start.7 = (bf16[32,1024]{1,0:T(8,128)(2,1)S(1)}, bf16[32,1024]{1,0:T(8,128)(2,1)}, u32[]{:S(2)}) copy-start(bf16[32,1024]{1,0:T(8,128)(2,1)} %bv_ref.1) | copy-start | bytes 196612
  2.5 9.5 %copy-start = (bf16[256,1024]{1,0:T(8,128)(2,1)S(1)}, bf16[256,1024]{1,0:T(8,128)(2,1)}, u32[]{:S(2)}) copy-start(bf16[256,1024]{1,0:T(8,128)(2,1)} %q_ref.1) | copy-start | bytes 1572868
  2.5 9.5 %copy-start.8 = (s32[16]{0:T(128)S(1)}, s32[16]{0:T(128)}, u32[]{:S(2)}) copy-start(s32[16]{0:T(128)} %lengths_ref.1) | copy-start | bytes 196
  2.5 9.5 %copy-start.9 = (s32[16]{0:T(128)S(1)}, s32[16]{0:T(128)}, u32[]{:S(2)}) copy-start(s32[16]{0:T(128)} %counts_ref.1) | copy-start | bytes 196
  12.0 9.4 %copy-start.4 = (bf16[256,1024]{1,0:T(8,128)(2,1)S(1)}, bf16[256,1024]{1,0:T(8,128)(2,1)}, u32[]{:S(2)}) copy-start(bf16[256,1024]{1,0:T(8,128)(2,1)} %wk_ref.1) | copy-start | bytes 1572868
  12.0 9.3 %copy-start.5 = (bf16[256,1024]{1,0:T(8,128)(2,1)S(1)}, bf16[256,1024]{1,0:T(8,128)(2,1)}, u32[]{:S(2)}) copy-start(bf16[256,1024]{1,0:T(8,128)(2,1)} %wv_ref.1) | copy-start | bytes 1572868
